TPU v7x, 128 devices: a whole 4x4x4 slice. The times are simulated.
128 devices in a mesh: dp: 16 (over y, z_hi, core), seq: 8 (over z_lo, x).
Axes of the slice: x: 4, y: 4, z: 4 (z_hi: 2, z_lo: 2; z = z_hi * 2 + z_lo), core: 2. Of those that a mesh axis runs over, the one named last changes fastest.
Arguments:
- prefix_hidden: bfloat16 [256, 816, 2048], P(('dp', 'seq')), may hold values from -24 to 24
- cameras: int32 [256], P(('dp', 'seq')), may hold values from 1 to 3, as said below
- text_length: int32 [256], P(('dp', 'seq')), may hold values from 1 to 48, as said below
- action_noise: bfloat16 [256, 50, 32], P(('dp', 'seq')), may hold values from -6 to 6
- clean_actions: bfloat16 [256, 50, 32], P(('dp', 'seq')), may hold values from -6 to 6
- flow_time: float32 [256], P(('dp', 'seq')), may hold values from 0.05 to 0.95
- input_weight: bfloat16 [32, 1024], replicated, may hold values from -1 to 1
- prefix_kv_weight: bfloat16 [2048, 512], P(('dp', 'seq')), may hold values from -2 to 2
- action_kv_weight: bfloat16 [1024, 512], P(('dp', 'seq')), may hold values from -2 to 2
- query_weight: bfloat16 [1024, 2048], P('dp', 'seq'), may hold values from -2 to 2
- cotangent: bfloat16 [256, 50, 2048], P(('dp', 'seq')), may hold values from -0.59765625 to 0.59765625
Outputs:
- attended: bfloat16 [256, 50, 2048], P(('dp', 'seq'))
- grad_query_weight: float32 [1024, 2048], P('dp', 'seq')
- grad_prefix_kv_weight: float32 [2048, 512], P(('dp', 'seq'))
- grad_action_kv_weight: float32 [1024, 512], P(('dp', 'seq'))
Inputs may be any that keep to these rules, and one draw needn't show every extreme that they name: Some sample has 3 cameras and some has 1. `text_length`: some sample has 48 prompt tokens and some has 1.
All inputs are finite; a program needn't handle non-finite values.
Results may differ from a plain program's by a relative error of at most 0.02.
The roundings to bfloat16 on the way count: a program that leaves them out, or rounds other values in their place, can miss the bound.
Values may be sent and summed in bfloat16 or wider, within the bound.
A program may use at most 128 MiB of HBM per device.

v0:
```python
import math

import jax
import jax.numpy as jnp
from jax import lax
from jax.sharding import PartitionSpec as P

IMG = 256


EPS = 1e-06


def rms_rounded(hidden):
    wide = hidden.astype(jnp.float32)
    return (wide * lax.rsqrt(jnp.mean(wide * wide, axis=-1, keepdims=True) + EPS)).astype(
        jnp.bfloat16
    )


def time_feature(flow_col, row_width):
    half_width = row_width // 2
    fraction = jnp.arange(half_width, dtype=jnp.float32) / (half_width - 1)
    period = 0.004 * 1000.0**fraction
    angle = flow_col[..., None] * (2.0 * math.pi / period)
    return jnp.concatenate([jnp.sin(angle), jnp.cos(angle)], axis=-1)


def row_fold(activ, piece):
    return jnp.dot(activ, piece, preferred_element_type=jnp.float32)


def left_product(activ, right_rows):
    return lax.dot_general(
        activ, right_rows, (((0,), (0,)), ((), ())), preferred_element_type=jnp.float32
    )


def project_query(action_norm, weight_rows):
    sample_count, step_count, row_width = action_norm.shape
    action_flat = action_norm.reshape(sample_count * step_count, row_width)
    summed = row_fold(action_flat, lax.all_gather(weight_rows, "dp", axis=0, tiled=True))
    return summed.astype(jnp.bfloat16).reshape(sample_count, step_count, weight_rows.shape[1])


def attend(query_rows, kv_rows, valid, cot_rows, groups):
    sample_count, step_count, row_width = query_rows.shape
    head_dim = kv_rows.shape[2] // 2
    head_count = row_width // head_dim
    inv_root = head_dim ** (-0.5)
    query_heads = query_rows.reshape(sample_count, step_count, head_count, head_dim)
    key_part = kv_rows[:, :, :head_dim]
    value_part = kv_rows[:, :, head_dim:]
    logits = (
        jnp.einsum("sahd,skd->shak", query_heads, key_part, preferred_element_type=jnp.float32)
        * inv_root
    )
    logits = jnp.where(valid[:, None, None, :], logits, -1e30)
    row_peak = jnp.max(logits, axis=-1, keepdims=True)
    expo_vals = jnp.exp(logits - row_peak)
    weights = expo_vals / jnp.sum(expo_vals, axis=-1, keepdims=True)
    weights_low = weights.astype(jnp.bfloat16)
    attended = jnp.einsum(
        "shak,skd->sahd", weights_low, value_part, preferred_element_type=jnp.float32
    )
    attended = attended.astype(jnp.bfloat16).reshape(sample_count, step_count, row_width)
    cot_heads = cot_rows.reshape(sample_count, step_count, head_count, head_dim)
    dprob = jnp.einsum("sahd,skd->shak", cot_heads, value_part, preferred_element_type=jnp.float32)
    row_inner = jnp.sum(weights * dprob, axis=-1, keepdims=True)
    dscore = (weights * (dprob - row_inner) * inv_root).astype(jnp.bfloat16)
    grad_query = jnp.einsum("shak,skd->sahd", dscore, key_part, preferred_element_type=jnp.float32)
    grad_query = grad_query.astype(jnp.bfloat16).reshape(sample_count, step_count, row_width)
    grad_keys = jnp.einsum(
        "shak,sahd->shkd", dscore, query_heads, preferred_element_type=jnp.float32
    )
    grad_values = jnp.einsum(
        "shak,sahd->shkd", weights_low, cot_heads, preferred_element_type=jnp.float32
    )
    key_value_grad = jnp.concatenate([grad_keys, grad_values], axis=-1)
    partial_value = key_value_grad.reshape(
        sample_count, groups, head_count // groups, kv_rows.shape[1], 2 * head_dim
    )
    return (attended, grad_query, jnp.sum(partial_value, axis=2))


def on_device(
    prefix_hidden,
    cameras,
    text_length,
    action_noise,
    clean_actions,
    flow_time,
    input_weight,
    prefix_kv_weight,
    action_kv_weight,
    query_weight,
    cotangent,
):
    sample_count, prefix_rows, model_width = prefix_hidden.shape
    step_count = action_noise.shape[1]
    expert_width = input_weight.shape[1]
    pair_width = prefix_kv_weight.shape[1]
    lengths = cameras * IMG + text_length
    prefix_norm = rms_rounded(prefix_hidden)
    prefix_flat = prefix_norm.reshape(sample_count * prefix_rows, model_width)
    prefix_kv = row_fold(
        prefix_flat, lax.all_gather(prefix_kv_weight, ("dp", "seq"), axis=0, tiled=True)
    )
    prefix_kv = prefix_kv.astype(jnp.bfloat16).reshape(sample_count, prefix_rows, pair_width)
    flow_col = flow_time[:, None, None]
    noisy = (
        flow_col * action_noise.astype(jnp.float32)
        + (1.0 - flow_col) * clean_actions.astype(jnp.float32)
    ).astype(jnp.bfloat16)
    action_wide = jnp.dot(
        noisy.reshape(sample_count * step_count, noisy.shape[2]),
        input_weight,
        preferred_element_type=jnp.float32,
    )
    action_wide = (
        action_wide.reshape(sample_count, step_count, expert_width)
        + time_feature(flow_time, expert_width)[:, None, :]
    )
    action_norm = rms_rounded(action_wide)
    action_flat = action_norm.reshape(sample_count * step_count, expert_width)
    action_kv = row_fold(
        action_flat, lax.all_gather(action_kv_weight, ("dp", "seq"), axis=0, tiled=True)
    )
    action_kv = action_kv.astype(jnp.bfloat16).reshape(sample_count, step_count, pair_width)
    kv_rows = jnp.concatenate([prefix_kv, action_kv], axis=1)
    positions = jnp.arange(prefix_rows + step_count, dtype=jnp.int32)
    valid = (positions[None, :] < lengths[:, None]) | (positions[None, :] >= prefix_rows)
    valid_low = valid.astype(jnp.bfloat16)
    group_kv, group_norm, group_valid = (
        lax.all_gather(kv_rows, "seq", axis=0, tiled=True),
        lax.all_gather(action_norm, "seq", axis=0, tiled=True),
        lax.all_gather(valid_low, "seq", axis=0, tiled=True),
    )
    group_cot = lax.all_to_all(cotangent, "seq", split_axis=2, concat_axis=0, tiled=True)
    query_rows = project_query(group_norm, query_weight)
    attended_heads, grad_query, partial_value = attend(
        query_rows, group_kv, group_valid > 0, group_cot, 1
    )
    attended = lax.all_to_all(attended_heads, "seq", split_axis=0, concat_axis=2, tiled=True)
    grad_kv = lax.psum_scatter(
        partial_value[:, 0].astype(jnp.bfloat16), "seq", scatter_dimension=0, tiled=True
    )
    group_flat = group_norm.reshape(-1, expert_width)
    query_flat = grad_query.reshape(group_flat.shape[0], -1)
    grad_query_weight = lax.psum_scatter(
        left_product(group_flat, query_flat), "dp", scatter_dimension=0, tiled=True
    )
    prefix_grad = grad_kv[:, :prefix_rows].reshape(-1, pair_width)
    action_grad = grad_kv[:, prefix_rows:].reshape(-1, pair_width)
    grad_prefix_kv_weight = lax.psum_scatter(
        left_product(prefix_flat, prefix_grad), ("dp", "seq"), scatter_dimension=0, tiled=True
    )
    grad_action_kv_weight = lax.psum_scatter(
        left_product(action_flat, action_grad), ("dp", "seq"), scatter_dimension=0, tiled=True
    )
    return (attended, grad_query_weight, grad_prefix_kv_weight, grad_action_kv_weight)


def solution(mesh):
    return jax.shard_map(
        on_device,
        mesh=mesh,
        in_specs=(
            P(("dp", "seq"), None, None),
            P(("dp", "seq")),
            P(("dp", "seq")),
            P(("dp", "seq"), None, None),
            P(("dp", "seq"), None, None),
            P(("dp", "seq")),
            P(),
            P(("dp", "seq"), None),
            P(("dp", "seq"), None),
            P("dp", "seq"),
            P(("dp", "seq"), None, None),
        ),
        out_specs=(
            P(("dp", "seq"), None, None),
            P("dp", "seq"),
            P(("dp", "seq"), None),
            P(("dp", "seq"), None),
        ),
        check_vma=False,
    )
```

profile of v0, /device:TPU:0, one launch (start us, length us, event | category | flops | bytes accessed | tf_op | source)
XLA Modules:
  0.0 2353.3 jit_solution(16116749612483145584)
XLA Ops:
  7.2 0.7 all-gather.8.cloned.1.call-update
  8.0 0.7 all-gather.6.cloned.1.call-update
  8.7 0.8 multiply_sine_fusion
  9.5 0.7 broadcast_subtract_fusion
  10.2 1.1 multiply_reduce_fusion
  11.3 0.8 multiply_convert_fusion
  12.2 1.0 reshape.126
  13.2 4.4 fusion
  17.7 0.4 copy-done.2
  18.0 3.9 fusion.1
  21.9 281.8 %all-gather.8.cloned.1.call-done = bf16[1024,512]{1,0:T(8,128)(2,1)} async-done(((bf16[8,512]{1,0:T(8,128)(2,1)}), bf16[1024,512]{1,0:T(8,128)(2,1)}) %all-gather.8.cloned.1.call-update) | async-done | bytes 1048592 | tf_op jit(solution)/shard_map/all_gather | solution.py:127
  303.7 1.5 convolution_convert_fusion.2
  305.2 301.3 %all-gather.6.cloned.1.call-done = bf16[2048,512]{1,0:T(8,128)(2,1)} async-done(((bf16[16,512]{1,0:T(8,128)(2,1)}), bf16[2048,512]{1,0:T(8,128)(2,1)}) %all-gather.6.cloned.1.call-update) | async-done | bytes 2097168 | tf_op jit(solution)/shard_map/all_gather | solution.py:107
  606.5 7.1 convolution_convert_fusion
  613.7 1.3 pad_maximum_fusion
  615.0 1.0 copy.23
  616.0 3.3 reshape.141
  619.3 5.6 all-to-all-start.1
  625.0 0.1 fusion.42
  625.0 33.9 %all-gather = bf16[8,2,866]{2,1,0:T(2,128)(2,1)S(1)} all-gather(bf16[1,2,866]{2,1,0:T(2,128)(2,1)S(1)} %fusion.42), channel_id=1, replica_groups=mesh['dp'=16,'seq'=8] {'seq'}, dimensions={0}, use_global_device_ids=true | all-gather | bytes 31176 | tf_op jit(solution)/shard_map/all_gather | solution.py:137
  659.0 157.4 %all_gather.23 = bf16[1024,256]{1,0:T(8,128)(2,1)S(1)} all-gather(bf16[64,256]{1,0:T(8,128)(2,1)S(1)} %copy-done.9), channel_id=1, replica_groups=mesh['dp'=16,'seq'=8] {'dp'}, dimensions={0}, use_global_device_ids=true | all-gather | bytes 557056 | tf_op jit(solution)/shard_map/all_gather | solution.py:42
  816.5 3.3 reshape.142
  819.8 1.9 copy.24
  821.6 1.7 reshape.128
  823.3 0.6 convolution_convert_fusion.1
  823.9 0.9 reshape.129
  824.8 5.2 bitcast_reduce_fusion
  830.1 1.0 fusion.16
  831.1 0.0 copy-done.7
  831.1 2.8 convert_bitcast_fusion
  833.9 4.5 fusion.10
  838.3 1.3 fusion.18
  839.7 2.1 convert_bitcast_fusion.1
  841.9 7.2 maximum_bitcast_fusion
  849.1 0.3 reduce-scatter.5.cloned.1.call-start
  849.4 6.1 fusion.30
  855.5 1.9 reshape_reshape.4
  857.4 3.2 fusion.45
  860.7 131.2 %reduce-scatter.7.cloned.1.call-done = bf16[2,866,512]{2,1,0:T(8,128)(2,1)} async-done(((bf16[16,866,512]{2,1,0:T(8,128)(2,1)}), bf16[2,866,512]{2,1,0:T(8,128)(2,1)}) %reduce-scatter.7.cloned.1.call-update) | async-done | bytes 1773584 | tf_op jit(solution)/shard_map/reduce_scatter | solution.py:145
  992.0 2.7 convolution_bitcast_fusion.1
  994.7 9.3 convolution_bitcast_fusion
  1004.1 4.6 fusion.33
  1008.7 12.1 all_to_all.33
  1020.8 0.1 copy.22
  1020.9 0.8 all_to_all.27
  1021.8 40.6 %reduce-scatter.5.cloned.1.call-done = f32[64,256]{1,0:T(8,128)} async-done(((f32[1024,256]{1,0:T(8,128)}), f32[64,256]{1,0:T(8,128)}) %reduce-scatter.5.cloned.1.call-update) | async-done | bytes 65552 | tf_op jit(solution)/shard_map/reduce_scatter | solution.py:150
  1062.3 642.1 %reduce-scatter.11.cloned.1.call-done = f32[8,512]{1,0:T(8,128)} async-done(((f32[1024,512]{1,0:T(8,128)}), f32[8,512]{1,0:T(8,128)}) %reduce-scatter.11.cloned.1.call-update) | async-done | bytes 16400 | tf_op jit(solution)/shard_map/reduce_scatter | solution.py:158
  1704.5 642.0 %reduce-scatter.9.cloned.1.call-done = f32[16,512]{1,0:T(8,128)} async-done(((f32[2048,512]{1,0:T(8,128)}), f32[16,512]{1,0:T(8,128)}) %reduce-scatter.9.cloned.1.call-update) | async-done | bytes 32784 | tf_op jit(solution)/shard_map/reduce_scatter | solution.py:155
  (47 shorter events, 0.6 us)
Async XLA Ops:
  7.2 3.0 copy-start
  7.2 296.5 %all-gather.8.cloned.1.call-start = ((), (), s32[]{:S(2)}) async-start(), calls=%async_computation.7 | async-start | bytes 1056768 | tf_op jit(solution)/shard_map/all_gather | solution.py:127
  7.9 598.6 %all-gather.6.cloned.1.call-start = ((), (), s32[]{:S(2)}) async-start(), calls=%async_computation.6 | async-start | bytes 2113536 | tf_op jit(solution)/shard_map/all_gather | solution.py:107
  8.7 813.0 %all-gather.12.cloned.1.call-start = ((), (), s32[]{:S(2)}) async-start(), calls=%async_computation.9 | async-start | bytes 2064384 | tf_op jit(solution)/shard_map/all_gather | solution.py:136
  12.2 812.7 %all-gather.10.cloned.1.call-start = ((), (), s32[]{:S(2)}) async-start(), calls=%async_computation.8 | async-start | bytes 16072704 | tf_op jit(solution)/shard_map/all_gather | solution.py:135
  13.2 4.8 copy-start.2
  613.6 1.4 copy-start.8
  615.0 9.9 copy-start.10
  615.0 9.9 copy-start.11
  615.0 44.0 %copy-start.9 = (bf16[64,256]{1,0:T(8,128)(2,1)S(1)}, bf16[64,256]{1,0:T(8,128)(2,1)}, u32[]{:S(2)}) copy-start(bf16[64,256]{1,0:T(8,128)(2,1)} %param.20) | copy-start | bytes 98308
  619.3 197.1 %all-to-all-start.1 = ((bf16[8,2,12800]{2,1,0:T(2,128)(2,1)}), bf16[8,2,12800]{2,1,0:T(2,128)(2,1)S(1)}, u32[]{:S(2)}, u32[]{:S(2)}) async-start(bf16[8,2,12800]{2,1,0:T(2,128)(2,1)} %reshape.141), calls=%async_computation.1 | async-start | bytes 819200 | tf_op jit(solution)/shard_map/all_to_all | solution.py:139
  624.9 367.1 %reduce-scatter.7.cloned.1.call-start = ((), (), s32[]{:S(2)}) async-start(), calls=%async_computation.11 | async-start | bytes 16072704 | tf_op jit(solution)/shard_map/reduce_scatter | solution.py:145
  823.3 1.5 copy-start.6
  830.1 1.0 copy-start.7
  838.3 1.4 copy-start.5
  839.7 2.2 copy-start.3
  849.1 213.2 %reduce-scatter.5.cloned.1.call-start = ((), (), s32[]{:S(2)}) async-start(), calls=%async_computation.10 | async-start | bytes 1114112 | tf_op jit(solution)/shard_map/reduce_scatter | solution.py:150
  857.4 134.6 %copy-start.4 = (bf16[2,50,1024]{2,1,0:T(8,128)(2,1)S(1)}, bf16[2,50,1024]{2,1,0:T(8,128)(2,1)}, u32[]{:S(2)}) copy-start(bf16[2,50,1024]{2,1,0:T(8,128)(2,1)} %multiply_convert_fusion) | copy-start | bytes 614404
  860.7 843.8 %reduce-scatter.11.cloned.1.call-start = ((), (), s32[]{:S(2)}) async-start(), calls=%async_computation.13 | async-start | bytes 2113536 | tf_op jit(solution)/shard_map/reduce_scatter | solution.py:158
  994.7 1351.8 %reduce-scatter.9.cloned.1.call-start = ((), (), s32[]{:S(2)}) async-start(), calls=%async_computation.12 | async-start | bytes 4227072 | tf_op jit(solution)/shard_map/reduce_scatter | solution.py:155
  1004.1 1342.4 %copy-start.1 = (bf16[32,1024]{1,0:T(8,128)(2,1)S(1)}, bf16[32,1024]{1,0:T(8,128)(2,1)}, u32[]{:S(2)}) copy-start(bf16[32,1024]{1,0:T(8,128)(2,1)} %param.17) | copy-start | bytes 196612
Sparse Core Ops, SparseCore 0:
  9.7 293.9 all-gather.7
  305.4 301.0 all-gather.5
  608.2 44.4 all-gather.11
  654.1 147.8 all-gather.9
  849.3 142.6 reduce-scatter.6
  996.7 65.5 reduce-scatter.4
  1065.3 639.1 reduce-scatter.10
  1707.5 638.9 reduce-scatter.8
where the time goes:
time: 2350 us
  waiting for transfers between devices  2040 us (87%)
  blocking collectives  203 us (9%)
  matrix products  50.9 us (2%)
    reduce_scatter x1, waiting for transfers between devices, on_device(): lax.psum_scatter(left_product(action_flat, action_grad), ('dp', 'seq'), s...  642 us
    reduce_scatter x1, waiting for transfers between devices, on_device(): lax.psum_scatter(left_product(prefix_flat, prefix_grad), ('dp', 'seq'), s...  642 us
    all_gather x1, waiting for transfers between devices, on_device(): lax.all_gather(prefix_kv_weight, ('dp', 'seq'), axis=0, tiled=True)  301 us
    all_gather x1, waiting for transfers between devices, on_device(): lax.all_gather(action_kv_weight, ('dp', 'seq'), axis=0, tiled=True)  282 us
    all_gather x1, blocking collectives, project_query(): lax.all_gather(weight_rows, 'dp', axis=0, tiled=True)  157 us
    reduce_scatter x1, waiting for transfers between devices, on_device(): lax.psum_scatter(partial_value[:, 0].astype(jnp.bfloat16), 'seq', scatter...  131 us
  transfers between devices with their start and end apart: 9, of which 6 were waited for; matrix products, arithmetic and copies ran while one was open for 3% of the time, Pallas kernels for 0%

commit v1 on v0

v1 whole, which is shorter than its diff:
```python
import math

import jax
import jax.numpy as jnp
from jax import lax
from jax.experimental import pallas as pl
from jax.experimental.pallas import tpu as pltpu
from jax.sharding import PartitionSpec as P

IMG = 256
EPS = 1e-06
MESH = pl.DeviceIdType.MESH
VMEM_LIMIT = 58 * 1024 * 1024
PREFIX, STEPS, PAD_STEPS, KEYS = 816, 50, 64, 896

ROWS = 48
ORDERS = ("xyz", "yzx", "zxy")
HALVES = (slice(0, 2), slice(2, 4))
FULL = slice(None)


class Place:
    def __init__(self):
        self.dp = lax.axis_index("dp")
        self.seq = lax.axis_index("seq")
        self.core = lax.rem(self.dp, 2)
        self.z_hi = lax.rem(self.dp // 2, 2)
        self.z_lo = self.seq // 4
        self.at = {
            "y": self.dp // 4,
            "z": self.z_hi * 2 + self.z_lo,
            "x": lax.rem(self.seq, 4),
        }
        self.sibling = self.device(core=1 - self.core)
        self.z_far = self.device(z=self.shifted("z", 2))

    def device(self, core=None, **moved):
        at = {**self.at, **moved}
        core = self.core if core is None else core
        return (
            at["y"] * 4 + (at["z"] // 2) * 2 + core,
            lax.rem(at["z"], 2) * 4 + at["x"],
        )

    def shifted(self, axis, by):
        return lax.rem(self.at[axis] + by, 4)

    def group_member(self, offset, sign=1):
        z_lo = lax.rem(self.z_lo + offset // 4, 2)
        x = lax.rem(self.at["x"] + sign * (offset % 4) + 4, 4)
        return z_lo * 4 + x

    def greet(self):
        barrier = pltpu.get_barrier_semaphore()
        others = [self.sibling, self.z_far]
        others += [(self.dp, self.group_member(offset)) for offset in range(1, 8)]
        others += [self.device(y=self.shifted("y", by)) for by in (1, 2, 3)]
        beyond = lax.rem(self.at["z"] + 3 + 2 * self.z_lo, 4)
        others.append(self.device(z=beyond))
        for other in others:
            pl.semaphore_signal(barrier, inc=1, device_id=other, device_id_type=MESH)
        pl.semaphore_wait(barrier, len(others))


class Links:
    def __init__(self, send_sem, recv_sem):
        self.send_sem, self.recv_sem = send_sem, recv_sem
        self.used = 0
        self.sent = []

    def slots(self, count):
        self.used += count
        return self.used - count

    def op(self, src, dst, to, slot):
        return pltpu.make_async_remote_copy(
            src_ref=src,
            dst_ref=dst,
            send_sem=self.send_sem.at[slot],
            recv_sem=self.recv_sem.at[slot],
            device_id=to,
            device_id_type=MESH,
        )

    def go(self, src, dst, to, slot):
        op = self.op(src, dst, to, slot)
        op.start()
        self.sent.append(op)

    def arrived(self, dst, to, slot):
        self.op(dst, dst, to, slot).wait_recv()


def run_together(works, tasks=()):
    live, tasks = list(works), list(tasks)
    while live or tasks:
        live = [work for work in live if next(work, "end") != "end"]
        if tasks:
            tasks.pop(0)()


def direct(links, place, axis, view, slot):
    own = place.at[axis]
    for by in (1, 3, 2):
        to = place.device(**{axis: place.shifted(axis, by)})
        links.go(view(own), view(own), to, slot + by - 1)
    yield
    for by in (1, 3, 2):
        links.arrived(view(place.shifted(axis, 4 - by)), place.sibling, slot + by - 1)


def ring(links, place, axis, view, slot, landed):
    own, right, left, across = (place.shifted(axis, by) for by in (0, 1, 3, 2))
    to_right, to_left = (place.device(**{axis: at}) for at in (right, left))
    links.go(view(own), view(own), to_right, slot)
    links.go(view(own), view(own), to_left, slot + 1)
    landed(own)
    yield
    links.arrived(view(left), to_right, slot)
    links.go(view(left, 0), view(left, 0), to_right, slot + 2)
    links.arrived(view(right), to_left, slot + 1)
    links.go(view(right, 1), view(right, 1), to_left, slot + 3)
    landed(left)
    landed(right)
    yield
    links.arrived(view(across, 0), to_right, slot + 2)
    links.arrived(view(across, 1), to_left, slot + 3)
    landed(across)


class Share:
    def __init__(self, links, place, view):
        self.links, self.place, self.view = links, place, view
        self.slot, self.due = links.slots(4), []

    def __call__(self, block):
        links, core = self.links, self.place.core
        slot = self.slot + len(self.due)
        mine = self.view(core, block)
        links.go(mine, mine, self.place.sibling, slot)
        self.due.append((self.view(1 - core, block), slot))

    def wait(self):
        for view, slot in self.due:
            self.links.arrived(view, self.place.sibling, slot)


def gather_part(links, place, ref, order):
    core = place.core
    first, second, third = order
    slot = links.slots(10)
    at = place.at
    yield from direct(
        links, place, first, lambda block: ref.at[core, at[third], at[second], block], slot
    )
    yield from direct(links, place, second, lambda block: ref.at[core, at[third], block], slot + 3)
    share = Share(links, place, lambda core, block: ref.at[core, block])

    def view(block, half=None):
        return ref.at[core, block] if half is None else ref.at[core, block, HALVES[half]]

    yield from ring(links, place, third, view, slot + 6, share)
    yield
    share.wait()


def gather_query(links, place, query_ref, then):
    core, y, z_hi = place.core, place.at["y"], place.z_hi
    slot = links.slots(5)
    links.go(query_ref.at[y, z_hi, core], query_ref.at[y, z_hi, core], place.z_far, slot)
    yield
    links.arrived(query_ref.at[y, 1 - z_hi, core], place.z_far, slot)
    share = Share(links, place, lambda core, block: query_ref.at[block, :, core])

    def view(block, half=None):
        return query_ref.at[block, FULL if half is None else half, core]

    yield from ring(links, place, "y", view, slot + 1, share)
    yield
    share.wait()
    then()


def reduce_ring(links, place, axis, pack, wire, half, fulls, slot):
    own, right, left, across = (place.shifted(axis, by) for by in (0, 1, 3, 2))
    to_right, to_left = (place.device(**{axis: at}) for at in (right, left))
    pack(across, 0)
    links.go(wire(across, 0), half.at[0], to_right, slot)
    pack(across, 1)
    links.go(wire(across, 1), half.at[1], to_left, slot + 1)
    yield
    pack(right, 1)
    links.go(wire(right, 1), fulls(0, 1), to_right, slot + 2)
    pack(left, 0)
    links.go(wire(left, 0), fulls(1, 0), to_left, slot + 3)
    yield
    links.arrived(half.at[0], to_right, slot)
    pack(right, 0, half.at[0])
    links.go(wire(right, 0), fulls(0, 0), to_right, slot + 4)
    links.arrived(half.at[1], to_left, slot + 1)
    pack(left, 1, half.at[1])
    links.go(wire(left, 1), fulls(1, 1), to_left, slot + 5)
    yield
    links.arrived(fulls(0, 1), to_right, slot + 2)
    links.arrived(fulls(1, 0), to_left, slot + 3)
    links.arrived(fulls(0, 0), to_right, slot + 4)
    links.arrived(fulls(1, 1), to_left, slot + 5)


def reduce_direct(links, place, axis, block_of, landing, slot):
    for by in (2, 1, 3):
        block = place.shifted(axis, by)
        links.go(
            block_of(block), landing.at[by - 1], place.device(**{axis: block}), slot + by - 1
        )
    yield
    for by in (1, 3, 2):
        links.arrived(landing.at[by - 1], place.sibling, slot + by - 1)


def reduce_part(links, place, grad_ref, pair_ref, v, part, finish):
    f32, bf16 = jnp.float32, jnp.bfloat16
    rows = slice(part * 16, part * 16 + 16)
    core = place.core
    first, second, third = ORDERS[part]
    wire, half, full = (v[f"{name}1_{part}"] for name in ("wire", "half", "full"))
    slot = links.slots(12)

    def mine(block, i, j):
        at = {first: block, second: i, third: j}
        y, z, x = at["y"], at["z"], at["x"]
        return grad_ref[y, z // 2, core, lax.rem(z, 2), x, rows, :] + pair_ref[y, z, x, rows, :]

    def pack(block, side, extra=None):
        for i in range(2):
            for j in range(4):
                value = mine(block, side * 2 + i, j)
                if extra is not None:
                    value = value + extra[i, j].astype(f32)
                wire[block, side * 2 + i, j] = value.astype(bf16)

    yield from reduce_ring(
        links, place, first, pack, lambda block, side: wire.at[block, HALVES[side]], half,
        lambda way, side: full.at[way, HALVES[side]], slot,
    )
    total, wire2, full2 = (v[f"{name}2_{part}"] for name in ("sum", "wire", "full"))
    for i in range(4):
        for j in range(4):
            value = mine(place.at[first], i, j)
            value = value + full[0, i, j].astype(f32) + full[1, i, j].astype(f32)
            total[i, j] = value
            wire2[i, j] = value.astype(bf16)
    yield from reduce_direct(links, place, second, lambda block: wire2.at[block], full2, slot + 6)
    total3, full3 = v[f"sum3_{part}"], v[f"full3_{part}"]
    value = total[place.at[second]]
    for k in range(3):
        value = value + full2[k].astype(f32)
    total3[...] = value
    yield from reduce_direct(links, place, third, lambda block: total3.at[block], full3, slot + 9)
    finish(total3[place.at[third]] + full3[0] + full3[1] + full3[2])


def reduce_query(links, place, first, v, out_ref):
    f32, bf16 = jnp.float32, jnp.bfloat16
    core, z_hi = place.core, place.z_hi
    grad_ref, pair_ref, wire = v["grad_query"], v["query_pair"], v["query_wire"]
    half, full, total, far_ref = v["query_half"], v["query_full"], v["query_sum"], v["query_far"]
    slot = links.slots(8)
    first()
    links.go(grad_ref.at[:, :, 1 - core], pair_ref, place.sibling, slot)
    yield
    links.arrived(pair_ref, place.sibling, slot)

    def pack(block, side, extra=None):
        value = grad_ref[block, side, core] + pair_ref[block, side]
        if extra is not None:
            value = value + extra[...].astype(f32)
        wire[block, side] = value.astype(bf16)

    yield from reduce_ring(
        links, place, "y", pack, lambda block, side: wire.at[block, side], half,
        lambda way, side: full.at[way, side], slot + 1,
    )
    own = place.at["y"]
    value = grad_ref[own, :, core] + pair_ref[own]
    total[...] = value + full[0].astype(f32) + full[1].astype(f32)
    links.go(total.at[1 - z_hi], far_ref, place.z_far, slot + 7)
    yield
    links.arrived(far_ref, place.z_far, slot + 7)
    out_ref[...] = total[z_hi] + far_ref[...]


def lanes_dot(left, right):
    return lax.dot_general(
        left, right, (((1,), (1,)), ((), ())), preferred_element_type=jnp.float32
    )


def rows_dot(left, right):
    return lax.dot_general(
        left, right, (((0,), (0,)), ((), ())), preferred_element_type=jnp.float32
    )


def dot(left, right):
    return jnp.dot(left, right, preferred_element_type=jnp.float32)


def step_kernel(
    cameras_ref, text_ref, hidden_ref, noisy_ref, time_ref, input_ref, cot_ref,
    own_prefix_ref, own_action_ref, own_query_ref,
    attended_ref, out_query_ref, out_prefix_ref, out_action_ref,
    v,
):
    f32, bf16 = jnp.float32, jnp.bfloat16
    place = Place()
    core, y, z_hi, z_lo, x = place.core, place.at["y"], place.z_hi, place.z_lo, place.at["x"]
    seq = place.seq
    links = Links(v["send"], v["recv"])

    loads = []
    for s in range(2):
        for i in range(3):
            rows = slice(i * 272, (i + 1) * 272)
            load = pltpu.make_async_copy(
                hidden_ref.at[s, rows, :], v["norm"].at[s, rows, :], v["load"].at[s * 3 + i]
            )
            load.start()
            loads.append(load)

    query_weight = v["query_weight"]
    own_action = own_action_ref[...].astype(f32)
    own_action = jnp.concatenate([own_action[:, 0:256], own_action[:, 256:512]], axis=0)
    own_parts = (own_prefix_ref[:, 0:256], own_prefix_ref[:, 256:512], own_action.astype(bf16))
    for part, (first, second, third) in enumerate(ORDERS):
        at = place.at
        v[f"weight_{part}"][core, at[third], at[second], at[first]] = own_parts[part]
    query_weight[y, z_hi, core] = own_query_ref[...]
    v["noisy"][seq] = noisy_ref[...]
    v["time"][seq] = time_ref[...]
    place.greet()

    packet = links.slots(16)
    for offset in range(1, 8):
        to = (place.dp, place.group_member(offset))
        links.go(noisy_ref, v["noisy"].at[seq], to, packet + offset)
        links.go(time_ref, v["time"].at[seq], to, packet + 8 + offset)

    act, act_t = v["act"], v["act_t"]

    def action_rows(offset):
        def run():
            member = place.group_member(offset, -1)
            if offset:
                to = (place.dp, member)
                links.arrived(v["noisy"].at[member], to, packet + offset)
                links.arrived(v["time"].at[member], to, packet + 8 + offset)
            wide = dot(v["noisy"][member][:, 0:32], input_ref[...])
            time = v["time"][member]
            pieces = []
            for s in range(2):
                rows = slice(s * PAD_STEPS, (s + 1) * PAD_STEPS)
                pieces.append(
                    jnp.concatenate(
                        [
                            wide[rows, i * 128 : (i + 1) * 128] + time[s * 8 + i : s * 8 + i + 1]
                            for i in range(8)
                        ],
                        axis=1,
                    )
                )
            wide = jnp.concatenate(pieces, axis=0)
            scale = lax.rsqrt(jnp.mean(wide * wide, axis=-1, keepdims=True) + EPS)
            rows = (wide * scale).astype(bf16)
            at = pl.ds(pl.multiple_of(member * 128, 128), 128)
            act[at, :] = rows
            act_t[:, at] = rows.T
            if offset == 0:
                row = lax.broadcasted_iota(jnp.int32, (128, 256), 0)
                col = lax.broadcasted_iota(jnp.int32, (128, 256), 1)
                within = col % 16
                origin = (col // 16) * 8 + within
                to_left = jnp.where((within < 8) & (row == origin), 1.0, 0.0).astype(bf16)
                to_right = jnp.where((within >= 8) & (row == origin - 8), 1.0, 0.0).astype(bf16)
                for i in range(8):
                    piece, cols = rows[:, i * 128 : (i + 1) * 128], slice(i * 256, (i + 1) * 256)
                    v["left"][:, cols] = dot(piece, to_left).astype(bf16)
                    v["right"][:, cols] = dot(piece, to_right).astype(bf16)

        return run

    def normalize(chunk):
        def run():
            loads[chunk].wait()
            s, start = chunk // 3, (chunk % 3) * 272

            def body(i, carry):
                at = pl.ds(pl.multiple_of(start + i * 16, 16), 16)
                wide = v["norm"][s, at, :].astype(f32)
                scale = lax.rsqrt(jnp.mean(wide * wide, axis=-1, keepdims=True) + EPS)
                v["norm"][s, at, :] = (wide * scale).astype(bf16)
                return carry

            lax.fori_loop(0, 17, body, 0)

        return run

    def place_cotangent():
        v["cot"][...] = jnp.zeros_like(v["cot"])
        for s in range(2):
            for h in range(8):
                v["cot"][h, s * PAD_STEPS : s * PAD_STEPS + STEPS, :] = cot_ref[
                    s, :, h * 256 : (h + 1) * 256
                ]

    exchange = links.slots(16)

    def send_queries():
        wide = query_weight[...].reshape(1024, 256)
        for offset in (1, 2, 3, 4, 5, 6, 7, 0):
            member = place.group_member(offset)
            at = pl.ds(pl.multiple_of(member * 128, 128), 128)
            value = dot(act[at, :], wide).astype(bf16)
            if offset:
                v["query_out"][offset] = value
                links.go(
                    v["query_out"].at[offset], v["query"].at[seq], (place.dp, member),
                    exchange + offset,
                )
            else:
                v["query"][seq] = value

    works = [gather_query(links, place, query_weight, send_queries)]
    works += [gather_part(links, place, v[f"weight_{part}"], ORDERS[part]) for part in range(3)]
    rows = [action_rows(offset) for offset in range(8)]
    tasks = [rows[0], lambda: [rows[i]() for i in (1, 3, 4)], lambda: [rows[i]() for i in (2, 5, 6, 7)]]
    tasks += [normalize(chunk) for chunk in range(6)] + [place_cotangent]
    run_together(works, tasks)

    wp, kv = v["wp"], v["kv"]

    def block_rows(part, a, b):
        ref, order = v[f"weight_{part}"], ORDERS[part][::-1]
        pieces = []
        for c in range(2):
            for low in range(2):
                at = {"y": a, "z": b * 2 + low}
                if order[2] == "x":
                    pieces.append(ref[c, at[order[0]], at[order[1]]].reshape(64, 256))
                else:
                    for col in range(4):
                        at["x"] = col
                        pieces.append(ref[c, at[order[0]], at[order[1]], at[order[2]]])
        return pieces

    def unpack(k, carry):
        keys, values = carry
        a, b = k // 2, lax.rem(k, 2)
        for part in range(2):
            start = k * 256
            for piece in block_rows(part, a, b):
                at = pl.ds(pl.multiple_of(start, 16), piece.shape[0])
                wp[at, part * 256 : (part + 1) * 256] = piece
                start += piece.shape[0]
        block = jnp.concatenate(block_rows(2, a, b), axis=0)
        at = pl.ds(pl.multiple_of(k * 256, 256), 256)
        return keys + dot(v["left"][:, at], block), values + dot(v["right"][:, at], block)

    zero = jnp.zeros((2 * PAD_STEPS, 256), f32)
    keys, values = lax.fori_loop(0, 8, unpack, (zero, zero))
    keys, values = keys.astype(bf16), values.astype(bf16)
    for s in range(2):
        rows = slice(s * PAD_STEPS, (s + 1) * PAD_STEPS)
        kv[s, PREFIX:KEYS, :] = jnp.zeros((KEYS - PREFIX, 512), bf16)
        kv[s, PREFIX : PREFIX + PAD_STEPS, 0:256] = keys[rows]
        kv[s, PREFIX : PREFIX + PAD_STEPS, 256:512] = values[rows]

    for s in range(2):

        def prefix(i, carry):
            at = pl.ds(pl.multiple_of(i * 272, 16), 272)
            kv[s, at, :] = dot(v["norm"][s, at, :], wp[...]).astype(bf16)
            return carry

        lax.fori_loop(0, 3, prefix, 0)

    for offset in range(1, 8):
        member = place.group_member(offset, -1)
        links.arrived(v["query"].at[member], (place.dp, member), exchange + offset)

    low_ref, ds_ref, gsum, gkv = v["low"], v["ds"], v["gsum"], v["gkv"]

    def sample(s, carry):
        length = cameras_ref[s] * IMG + text_ref[s]
        mine = pl.ds(pl.multiple_of(s * PAD_STEPS, PAD_STEPS), PAD_STEPS)

        def half(i, carry):
            heads = pl.ds(i * 4, 4)
            query = v["query"][heads, mine, :].reshape(256, 256)
            cot = v["cot"][heads, mine, :].reshape(256, 256)
            key, value = kv[s, :, 0:256], kv[s, :, 256:512]
            column = lax.broadcasted_iota(jnp.int32, (256, KEYS), 1)
            valid = (column < length) | ((column >= PREFIX) & (column < PREFIX + STEPS))
            logits = jnp.where(valid, lanes_dot(query, key) * 0.0625, -1e30)
            expo = jnp.exp(logits - jnp.max(logits, axis=-1, keepdims=True))
            probs = expo / jnp.sum(expo, axis=-1, keepdims=True)
            low = probs.astype(bf16)
            low_ref[...] = low
            dprob = lanes_dot(cot, value)
            inner = jnp.sum(probs * dprob, axis=-1, keepdims=True)
            dscore = (probs * (dprob - inner) * 0.0625).astype(bf16)
            ds_ref[...] = dscore
            attended = dot(low, value).astype(bf16)
            for j in range(4):
                at = pl.ds(pl.multiple_of((i * 4 + j) * 256, 256), 256)
                attended_ref[s, :, at] = attended[j * 64 : j * 64 + STEPS]
            v["gq"][heads, mine, :] = dot(dscore, key).astype(bf16).reshape(4, 64, 256)
            for j in range(4):
                rows = slice(j * 64, (j + 1) * 64)
                gsum[0:256, :] += rows_dot(query[rows], ds_ref[rows, :]).astype(bf16).astype(f32)
                gsum[256:512, :] += rows_dot(cot[rows], low_ref[rows, :]).astype(bf16).astype(f32)
            return carry

        gsum[...] = jnp.zeros_like(gsum)
        lax.fori_loop(0, 2, half, 0)
        gkv[s] = gsum[...].astype(bf16)
        return carry

    lax.fori_loop(0, 2, sample, 0)

    for offset in range(1, 8):
        member = place.group_member(offset)
        links.go(
            v["gq"].at[member], v["group_gq"].at[seq], (place.dp, member), exchange + 8 + offset
        )
    v["group_gq"][seq] = v["gq"][seq]

    for s in range(2):
        turned = gkv[s, :, PREFIX - 48 : KEYS].astype(f32).T[48 : 48 + PAD_STEPS]
        ds_ref[s * 64 : (s + 1) * 64, 0:512] = turned.astype(bf16)
    grad, pair = v["grad"], v["pair"]
    pairing = links.slots(8)

    def pair_op(k):
        a, b = k // 2, lax.rem(k, 2)
        return links.op(
            grad.at[a, b, 1 - core], pair.at[a, pl.ds(b * 2, 2)], place.sibling, pairing + k
        )

    def grad_prefix(k, carry):
        at = pl.ds(pl.multiple_of(k * 256, 256), 256)
        a, b = k // 2, lax.rem(k, 2)
        value = dot(gkv[0, :, 0:PREFIX], v["norm"][0, :, at])
        value += dot(gkv[1, :, 0:PREFIX], v["norm"][1, :, at])
        value = value.T
        grad[a, b, :, :, :, 0:16, :] = value[:, 0:256].reshape(2, 2, 4, 16, 256)
        grad[a, b, :, :, :, 16:32, :] = value[:, 256:512].reshape(2, 2, 4, 16, 256)
        action = rows_dot(v["left"][:, at], ds_ref[0:128, 0:256])
        action += rows_dot(v["right"][:, at], ds_ref[0:128, 256:512])
        grad[a, b, :, :, :, 32:48, :] = action.reshape(2, 2, 4, 16, 256)
        pair_op(k).start()
        return carry

    lax.fori_loop(0, 8, grad_prefix, 0)
    for k in range(8):
        pair_op(k).wait_recv()

    def grad_query():
        for offset in range(1, 8):
            member = place.group_member(offset, -1)
            links.arrived(v["group_gq"].at[member], (place.dp, member), exchange + 8 + offset)
        rows = v["group_gq"][...].reshape(1024, 256)
        for a in range(4):
            value = dot(act_t[a * 256 : (a + 1) * 256, :], rows)
            v["grad_query"][a] = value.reshape(2, 2, 64, 256)

    def finish(part):
        def store(value):
            if part == 2:
                out_action_ref[:, 0:256] = value[0:8]
                out_action_ref[:, 256:512] = value[8:16]
            else:
                out_prefix_ref[:, part * 256 : (part + 1) * 256] = value

        return store

    works = [reduce_part(links, place, grad, pair, v, part, finish(part)) for part in range(3)]
    works.append(reduce_query(links, place, grad_query, v, out_query_ref))
    run_together(works)
    for op in links.sent:
        op.wait_send()
    for k in range(8):
        pair_op(k).wait_send()


def step(cameras, text_length, hidden, noisy, time, input_weight, cot, own_prefix, own_action, own_query):
    bf16, f32 = jnp.bfloat16, jnp.float32
    smem, vmem = pl.BlockSpec(memory_space=pltpu.SMEM), pl.BlockSpec(memory_space=pltpu.VMEM)
    scratch = dict(
        norm=pltpu.VMEM((2, PREFIX, 2048), bf16),
        query_weight=pltpu.VMEM((4, 2, 2, 64, 256), bf16),
        noisy=pltpu.VMEM((8, 128, 128), bf16),
        time=pltpu.VMEM((8, 16, 128), f32),
        act=pltpu.VMEM((1024, 1024), bf16),
        act_t=pltpu.VMEM((1024, 1024), bf16),
        left=pltpu.VMEM((128, 2048), bf16),
        right=pltpu.VMEM((128, 2048), bf16),
        cot=pltpu.VMEM((8, 128, 256), bf16),
        query=pltpu.VMEM((8, 128, 256), bf16),
        query_out=pltpu.VMEM((8, 128, 256), bf16),
        gq=pltpu.VMEM((8, 128, 256), bf16),
        group_gq=pltpu.VMEM((8, 128, 256), bf16),
        wp=pltpu.VMEM((2048, 512), bf16),
        kv=pltpu.VMEM((2, KEYS, 512), bf16),
        low=pltpu.VMEM((256, KEYS), bf16),
        ds=pltpu.VMEM((256, KEYS), bf16),
        gsum=pltpu.VMEM((512, KEYS), f32),
        gkv=pltpu.VMEM((2, 512, KEYS), bf16),
        grad=pltpu.VMEM((4, 2, 2, 2, 4, ROWS, 256), f32),
        pair=pltpu.VMEM((4, 4, 4, ROWS, 256), f32),
        grad_query=pltpu.VMEM((4, 2, 2, 64, 256), f32),
        query_pair=pltpu.VMEM((4, 2, 64, 256), f32),
        query_wire=pltpu.VMEM((4, 2, 64, 256), bf16),
        query_half=pltpu.VMEM((2, 64, 256), bf16),
        query_full=pltpu.VMEM((2, 2, 64, 256), bf16),
        query_sum=pltpu.VMEM((2, 64, 256), f32),
        query_far=pltpu.VMEM((64, 256), f32),
        send=pltpu.SemaphoreType.DMA((192,)),
        recv=pltpu.SemaphoreType.DMA((192,)),
        load=pltpu.SemaphoreType.DMA((6,)),
    )
    for part in range(3):
        scratch[f"weight_{part}"] = pltpu.VMEM((2, 4, 4, 4, 16, 256), bf16)
        scratch[f"wire1_{part}"] = pltpu.VMEM((4, 4, 4, 16, 256), bf16)
        scratch[f"half1_{part}"] = pltpu.VMEM((2, 2, 4, 16, 256), bf16)
        scratch[f"full1_{part}"] = pltpu.VMEM((2, 4, 4, 16, 256), bf16)
        scratch[f"sum2_{part}"] = pltpu.VMEM((4, 4, 16, 256), f32)
        scratch[f"wire2_{part}"] = pltpu.VMEM((4, 4, 16, 256), bf16)
        scratch[f"full2_{part}"] = pltpu.VMEM((3, 4, 16, 256), bf16)
        scratch[f"sum3_{part}"] = pltpu.VMEM((4, 16, 256), f32)
        scratch[f"full3_{part}"] = pltpu.VMEM((3, 16, 256), f32)
    return pl.pallas_call(
        step_kernel,
        out_shape=(
            jax.ShapeDtypeStruct((2, STEPS, 2048), bf16),
            jax.ShapeDtypeStruct((64, 256), f32),
            jax.ShapeDtypeStruct((16, 512), f32),
            jax.ShapeDtypeStruct((8, 512), f32),
        ),
        in_specs=[smem] * 2 + [pl.BlockSpec(memory_space=pl.ANY)] + [vmem] * 7,
        out_specs=(vmem,) * 4,
        scratch_shapes=[scratch],
        compiler_params=pltpu.CompilerParams(
            collective_id=1, has_side_effects=True, vmem_limit_bytes=VMEM_LIMIT
        ),
        cost_estimate=pl.CostEstimate(
            flops=10**10, bytes_accessed=9 * 10**6, transcendentals=10**6
        ),
        name="step",
    )(
        cameras, text_length, hidden, noisy, time, input_weight, cot,
        own_prefix, own_action, own_query,
    )


def time_feature(flow_col, row_width):
    half_width = row_width // 2
    fraction = jnp.arange(half_width, dtype=jnp.float32) / (half_width - 1)
    period = 0.004 * 1000.0**fraction
    angle = flow_col[..., None] * (2.0 * math.pi / period)
    return jnp.concatenate([jnp.sin(angle), jnp.cos(angle)], axis=-1)


def on_device(
    prefix_hidden,
    cameras,
    text_length,
    action_noise,
    clean_actions,
    flow_time,
    input_weight,
    prefix_kv_weight,
    action_kv_weight,
    query_weight,
    cotangent,
):
    flow_col = flow_time[:, None, None]
    noisy = (
        flow_col * action_noise.astype(jnp.float32)
        + (1.0 - flow_col) * clean_actions.astype(jnp.float32)
    ).astype(jnp.bfloat16)
    noisy = jnp.pad(noisy, ((0, 0), (0, PAD_STEPS - STEPS), (0, 96))).reshape(128, 128)
    time = time_feature(flow_time, 1024).reshape(16, 128)
    return step(
        cameras,
        text_length,
        prefix_hidden,
        noisy,
        time,
        input_weight,
        cotangent,
        prefix_kv_weight,
        action_kv_weight,
        query_weight,
    )


def solution(mesh):
    return jax.shard_map(
        on_device,
        mesh=mesh,
        in_specs=(
            P(("dp", "seq"), None, None),
            P(("dp", "seq")),
            P(("dp", "seq")),
            P(("dp", "seq"), None, None),
            P(("dp", "seq"), None, None),
            P(("dp", "seq")),
            P(),
            P(("dp", "seq"), None),
            P(("dp", "seq"), None),
            P("dp", "seq"),
            P(("dp", "seq"), None, None),
        ),
        out_specs=(
            P(("dp", "seq"), None, None),
            P("dp", "seq"),
            P(("dp", "seq"), None),
            P(("dp", "seq"), None),
        ),
        check_vma=False,
    )
```

time: 2350 us -> 96.6 us (0.04)
  waiting for transfers between devices: 2040 us -> 0 us
  blocking collectives: 203 us -> 0 us
  Pallas kernels: 0 us -> 83.6 us
  matrix products: 50.9 us -> 0 us
    reduce_scatter x4 -> x0, waiting for transfers between devices: 1460 us -> none  [the longest x1 642 us: on_device(): lax.psum_scatter(left_product(action_flat, action_grad), ('dp', 'seq'), s...]
    all_gather x4 -> x0, waiting for transfers between devices: 583 us -> none  [the longest x1 301 us: on_device(): lax.all_gather(prefix_kv_weight, ('dp', 'seq'), axis=0, tiled=True)]
    all_gather x2 -> x0, blocking collectives: 191 us -> none  [the longest x1 157 us: project_query(): lax.all_gather(weight_rows, 'dp', axis=0, tiled=True)]
    pallas_call x0 -> x1, Pallas kernels: none -> 83.6 us  [step(): pl.pallas_call(step_kernel, out_shape=(jax.ShapeDtypeStruct((2, STEPS, 20...]
    dot_general x13 -> x0, matrix products: 50.9 us -> none  [the longest x3 15.2 us: left_product(): lax.dot_general(activ, right_rows, (((0,), (0,)), ((), ())), preferred_el...]
  transfers between devices with their start and end apart: 9 -> 0, of which waited for: 6 -> 0; matrix products, arithmetic and copies ran while one was open for 3% -> 0% of each run, Pallas kernels for 0% -> 0%
where the time goes in v1:
time: 96.6 us; the launch traced here: 96.2 us
  Pallas kernels  83.6 us (87%)
  local copies, waits for them, and re-layouts  9.61 us (10%)
  other arithmetic  2.3 us (2%)
    pallas_call x1, Pallas kernels, step(): pl.pallas_call(step_kernel, out_shape=(jax.ShapeDtypeStruct((2, STEPS, 20...  83.6 us
    unnamed x5, local copies, waits for them, and re-layouts  6.18 us
    pallas_call x1, local copies, waits for them, and re-layouts, step(): pl.pallas_call(step_kernel, out_shape=(jax.ShapeDtypeStruct((2, STEPS, 20...  2.19 us

profile of v1, /device:TPU:0, one launch (start us, length us, event | category | flops | bytes accessed | tf_op | source)
XLA Modules:
  0.0 96.2 jit_solution(6883590530461226936)
XLA Ops:
  0.6 0.7 broadcast_subtract_fusion
  1.3 0.8 multiply_sine_fusion
  2.1 0.6 reshape.26.time_ref
  2.7 0.8 add_convert_fusion
  3.5 0.1 copy.18
  3.7 0.6 pad.4.clone
  4.3 1.9 %copy.16.cot_ref = bf16[2,50,2048]{2,1,0:T(8,128)(2,1)} copy(bf16[2,50,2048]{2,0,1:T(2,128)(2,1)} %param.21) | data formatting | bytes 819200 | tf_op args[10]
  6.2 83.6 %step.1 = (bf16[2,50,2048]{2,1,0:T(8,128)(2,1)}, f32[64,256]{1,0:T(8,128)}, f32[16,512]{1,0:T(8,128)}, f32[8,512]{1,0:T(8,128)}) custom-call(s32[2]{0:T(128)} %cameras_ref.1, s32[2]{0:T(128)} %text_ref.1, bf16[2,816,2048]{2,1,0:T(8,128)(2,1)} %hidden_ref.1, bf16[128,128]{1,0:T(8,128)(2,1)} %bitcast.1, f32[16,128]{1,0:T(8,128)} %reshape.26.time_ref, ...), custom_call_target="tpu_custom_call" | custom-call | flops 10000000000 | bytes 9000000 | tf_op jit(solution)/shard_map/step/pallas_call | solution.py:642
  89.8 2.2 %copy.17 = bf16[2,50,2048]{2,0,1:T(2,128)(2,1)} copy(bf16[2,50,2048]{2,1,0:T(8,128)(2,1)} %get-tuple-element.4) | data formatting | bytes 819200 | tf_op jit(solution)/shard_map/step/pallas_call | solution.py:642
  92.0 1.5 %copy.22 = f32[64,256]{1,0:T(8,128)} copy(f32[64,256]{1,0:T(8,128)} %get-tuple-element.15) | data formatting | bytes 131072
  93.5 1.4 %copy.23 = f32[16,512]{1,0:T(8,128)} copy(f32[16,512]{1,0:T(8,128)} %get-tuple-element.16) | data formatting | bytes 65536
  94.8 1.3 %copy.24 = f32[8,512]{1,0:T(8,128)} copy(f32[8,512]{1,0:T(8,128)} %get-tuple-element.17) | data formatting | bytes 32768
  (2 shorter events, 0.0 us)

commit v2 on v1

--- a/solution.py
+++ b/solution.py
@@ -307,7 +307,7 @@
 
 
 def step_kernel(
-    cameras_ref, text_ref, hidden_ref, noisy_ref, time_ref, input_ref, cot_ref,
+    cameras_ref, text_ref, flow_ref, hidden_ref, noise_ref, clean_ref, time_ref, input_ref, cot_ref,
     own_prefix_ref, own_action_ref, own_query_ref,
     attended_ref, out_query_ref, out_prefix_ref, out_action_ref,
     v,
@@ -318,15 +318,17 @@
     seq = place.seq
     links = Links(v["send"], v["recv"])
 
+    norm = v["norm"]
     loads = []
-    for s in range(2):
-        for i in range(3):
-            rows = slice(i * 272, (i + 1) * 272)
-            load = pltpu.make_async_copy(
-                hidden_ref.at[s, rows, :], v["norm"].at[s, rows, :], v["load"].at[s * 3 + i]
-            )
-            load.start()
-            loads.append(load)
+    chunks = [(s, start, count) for s in range(2) for start, count in ((0, 288), (288, 288), (576, 240))]
+    for k, (s, start, count) in enumerate(chunks):
+        load = pltpu.make_async_copy(
+            hidden_ref.at[s, pl.ds(start, count), :],
+            norm.at[pl.ds(s * KEYS + start, count), :],
+            v["load"].at[k],
+        )
+        load.start()
+        loads.append(load)
 
     query_weight = v["query_weight"]
     own_action = own_action_ref[...].astype(f32)
@@ -336,14 +338,23 @@
         at = place.at
         v[f"weight_{part}"][core, at[third], at[second], at[first]] = own_parts[part]
     query_weight[y, z_hi, core] = own_query_ref[...]
-    v["noisy"][seq] = noisy_ref[...]
+    turn, own_noisy = v["turn"], v["own_noisy"]
+    turn[...] = jnp.zeros_like(turn)
+    own_noisy[...] = jnp.zeros_like(own_noisy)
+    for s in range(2):
+        t = flow_ref[s]
+        turn[:, 0:STEPS] = t * noise_ref[s].astype(f32) + (1.0 - t) * clean_ref[s].astype(f32)
+        own_noisy[s * PAD_STEPS : (s + 1) * PAD_STEPS, 0:32] = (
+            turn[...].T[0:PAD_STEPS].astype(bf16)
+        )
+    v["noisy"][seq] = own_noisy[...]
     v["time"][seq] = time_ref[...]
     place.greet()
 
     packet = links.slots(16)
     for offset in range(1, 8):
         to = (place.dp, place.group_member(offset))
-        links.go(noisy_ref, v["noisy"].at[seq], to, packet + offset)
+        links.go(own_noisy, v["noisy"].at[seq], to, packet + offset)
         links.go(time_ref, v["time"].at[seq], to, packet + 8 + offset)
 
     act, act_t = v["act"], v["act_t"]
@@ -392,25 +403,33 @@
     def normalize(chunk):
         def run():
             loads[chunk].wait()
-            s, start = chunk // 3, (chunk % 3) * 272
+            s, start, count = chunks[chunk]
 
             def body(i, carry):
-                at = pl.ds(pl.multiple_of(start + i * 16, 16), 16)
-                wide = v["norm"][s, at, :].astype(f32)
-                scale = lax.rsqrt(jnp.mean(wide * wide, axis=-1, keepdims=True) + EPS)
-                v["norm"][s, at, :] = (wide * scale).astype(bf16)
+                places = [
+                    pl.ds(pl.multiple_of(s * KEYS + start + i * 48 + j * 16, 16), 16)
+                    for j in range(3)
+                ]
+                scales = []
+                for at in places:
+                    wide = norm[at, :].astype(f32)
+                    scales.append(lax.rsqrt(jnp.mean(wide * wide, axis=-1, keepdims=True) + EPS))
+                for at, scale in zip(places, scales):
+                    norm[at, :] = (norm[at, :].astype(f32) * scale).astype(bf16)
                 return carry
 
-            lax.fori_loop(0, 17, body, 0)
+            lax.fori_loop(0, count // 48, body, 0)
 
         return run
 
     def place_cotangent():
         v["cot"][...] = jnp.zeros_like(v["cot"])
         for s in range(2):
+            norm[s * KEYS + PREFIX : (s + 1) * KEYS, :] = jnp.zeros((KEYS - PREFIX, 2048), bf16)
+        for s in range(2):
             for h in range(8):
                 v["cot"][h, s * PAD_STEPS : s * PAD_STEPS + STEPS, :] = cot_ref[
-                    s, :, h * 256 : (h + 1) * 256
+                    :, s, h * 256 : (h + 1) * 256
                 ]
 
     exchange = links.slots(16)
@@ -469,61 +488,80 @@
     zero = jnp.zeros((2 * PAD_STEPS, 256), f32)
     keys, values = lax.fori_loop(0, 8, unpack, (zero, zero))
     keys, values = keys.astype(bf16), values.astype(bf16)
+
+    def prefix(i, carry):
+        at = pl.ds(pl.multiple_of(i * 256, 256), 256)
+        kv[at, :] = dot(norm[at, :], wp[...]).astype(bf16)
+        return carry
+
+    lax.fori_loop(0, 7, prefix, 0)
     for s in range(2):
         rows = slice(s * PAD_STEPS, (s + 1) * PAD_STEPS)
-        kv[s, PREFIX:KEYS, :] = jnp.zeros((KEYS - PREFIX, 512), bf16)
-        kv[s, PREFIX : PREFIX + PAD_STEPS, 0:256] = keys[rows]
-        kv[s, PREFIX : PREFIX + PAD_STEPS, 256:512] = values[rows]
-
-    for s in range(2):
-
-        def prefix(i, carry):
-            at = pl.ds(pl.multiple_of(i * 272, 16), 272)
-            kv[s, at, :] = dot(v["norm"][s, at, :], wp[...]).astype(bf16)
-            return carry
-
-        lax.fori_loop(0, 3, prefix, 0)
+        start = s * KEYS + PREFIX
+        kv[start : start + PAD_STEPS, 0:256] = keys[rows]
+        kv[start : start + PAD_STEPS, 256:512] = values[rows]
 
     for offset in range(1, 8):
         member = place.group_member(offset, -1)
         links.arrived(v["query"].at[member], (place.dp, member), exchange + offset)
 
-    low_ref, ds_ref, gsum, gkv = v["low"], v["ds"], v["gsum"], v["gkv"]
+    low_ref, ds_ref, gkv = v["low"], v["ds"], v["gkv"]
+    logits_ref, dprob_ref = v["logits"], v["dprob"]
+
+    def sixteenth(rows):
+        return (rows.astype(f32) * 0.0625).astype(bf16)
 
     def sample(s, carry):
         length = cameras_ref[s] * IMG + text_ref[s]
         mine = pl.ds(pl.multiple_of(s * PAD_STEPS, PAD_STEPS), PAD_STEPS)
-
-        def half(i, carry):
-            heads = pl.ds(i * 4, 4)
+        start = pl.multiple_of(s * KEYS, 128)
+        tokens = pl.ds(start, KEYS)
+        column = lax.broadcasted_iota(jnp.int32, (1, KEYS), 1)
+        valid = (column < length) | ((column >= PREFIX) & (column < PREFIX + STEPS))
+        bias = jnp.where(valid, 0.0, -1e30)
+        for i in range(2):
+            heads = slice(i * 4, i * 4 + 4)
+            half = slice(i * 256, (i + 1) * 256)
             query = v["query"][heads, mine, :].reshape(256, 256)
             cot = v["cot"][heads, mine, :].reshape(256, 256)
-            key, value = kv[s, :, 0:256], kv[s, :, 256:512]
-            column = lax.broadcasted_iota(jnp.int32, (256, KEYS), 1)
-            valid = (column < length) | ((column >= PREFIX) & (column < PREFIX + STEPS))
-            logits = jnp.where(valid, lanes_dot(query, key) * 0.0625, -1e30)
-            expo = jnp.exp(logits - jnp.max(logits, axis=-1, keepdims=True))
-            probs = expo / jnp.sum(expo, axis=-1, keepdims=True)
-            low = probs.astype(bf16)
-            low_ref[...] = low
-            dprob = lanes_dot(cot, value)
-            inner = jnp.sum(probs * dprob, axis=-1, keepdims=True)
-            dscore = (probs * (dprob - inner) * 0.0625).astype(bf16)
-            ds_ref[...] = dscore
-            attended = dot(low, value).astype(bf16)
+            logits_ref[...] = lanes_dot(sixteenth(query), kv[tokens, 0:256])
+            dprob_ref[...] = lanes_dot(sixteenth(cot), kv[tokens, 256:512])
+
+            def softmax(b, carry):
+                at = pl.ds(pl.multiple_of(b * 16, 16), 16)
+                to = pl.ds(pl.multiple_of(i * 256 + b * 16, 16), 16)
+                logits = logits_ref[at, :] + bias
+                expo = jnp.exp(logits - jnp.max(logits, axis=-1, keepdims=True))
+                probs = expo * (1.0 / jnp.sum(expo, axis=-1, keepdims=True))
+                low_ref[to, :] = probs.astype(bf16)
+                dprob = dprob_ref[at, :]
+                inner = jnp.sum(probs * dprob, axis=-1, keepdims=True)
+                ds_ref[to, :] = (probs * (dprob - inner)).astype(bf16)
+                return carry
+
+            lax.fori_loop(0, 16, softmax, 0, unroll=4)
+            attended = dot(low_ref[half, :], kv[tokens, 256:512]).astype(bf16)
             for j in range(4):
-                at = pl.ds(pl.multiple_of((i * 4 + j) * 256, 256), 256)
+                at = slice((i * 4 + j) * 256, (i * 4 + j + 1) * 256)
                 attended_ref[s, :, at] = attended[j * 64 : j * 64 + STEPS]
-            v["gq"][heads, mine, :] = dot(dscore, key).astype(bf16).reshape(4, 64, 256)
-            for j in range(4):
-                rows = slice(j * 64, (j + 1) * 64)
-                gsum[0:256, :] += rows_dot(query[rows], ds_ref[rows, :]).astype(bf16).astype(f32)
-                gsum[256:512, :] += rows_dot(cot[rows], low_ref[rows, :]).astype(bf16).astype(f32)
+            grad = dot(ds_ref[half, :], kv[tokens, 0:256]).astype(bf16)
+            v["gq"][heads, mine, :] = grad.reshape(4, 64, 256)
+        for h in range(8):
+            v["query_t"][h] = v["query"][h, mine, :].T
+            v["cot_t"][h] = v["cot"][h, mine, :].T
+
+        def tile(t, carry):
+            at = pl.ds(pl.multiple_of(t * 128, 128), 128)
+            to = pl.ds(pl.multiple_of(s * KEYS + t * 128, 128), 128)
+            for left, right, top in ((v["query_t"], ds_ref, 0), (v["cot_t"], low_ref, 256)):
+                total = jnp.zeros((256, 128), f32)
+                for h in range(8):
+                    term = dot(left[h], right[h * 64 : (h + 1) * 64, at])
+                    total = total + term.astype(bf16).astype(f32)
+                gkv[top : top + 256, to] = total.astype(bf16)
             return carry
 
-        gsum[...] = jnp.zeros_like(gsum)
-        lax.fori_loop(0, 2, half, 0)
-        gkv[s] = gsum[...].astype(bf16)
+        lax.fori_loop(0, 7, tile, 0)
         return carry
 
     lax.fori_loop(0, 2, sample, 0)
@@ -536,7 +574,7 @@
     v["group_gq"][seq] = v["gq"][seq]
 
     for s in range(2):
-        turned = gkv[s, :, PREFIX - 48 : KEYS].astype(f32).T[48 : 48 + PAD_STEPS]
+        turned = gkv[:, s * KEYS + PREFIX - 48 : (s + 1) * KEYS].astype(f32).T[48 : 48 + PAD_STEPS]
         ds_ref[s * 64 : (s + 1) * 64, 0:512] = turned.astype(bf16)
     grad, pair = v["grad"], v["pair"]
     pairing = links.slots(8)
@@ -550,8 +588,7 @@
     def grad_prefix(k, carry):
         at = pl.ds(pl.multiple_of(k * 256, 256), 256)
         a, b = k // 2, lax.rem(k, 2)
-        value = dot(gkv[0, :, 0:PREFIX], v["norm"][0, :, at])
-        value += dot(gkv[1, :, 0:PREFIX], v["norm"][1, :, at])
+        value = dot(gkv[...], norm[:, at])
         value = value.T
         grad[a, b, :, :, :, 0:16, :] = value[:, 0:256].reshape(2, 2, 4, 16, 256)
         grad[a, b, :, :, :, 16:32, :] = value[:, 256:512].reshape(2, 2, 4, 16, 256)
@@ -593,11 +630,13 @@
         pair_op(k).wait_send()
 
 
-def step(cameras, text_length, hidden, noisy, time, input_weight, cot, own_prefix, own_action, own_query):
+def step(cameras, text_length, flow_time, hidden, noise, clean, time, input_weight, cot, own_prefix, own_action, own_query):
     bf16, f32 = jnp.bfloat16, jnp.float32
     smem, vmem = pl.BlockSpec(memory_space=pltpu.SMEM), pl.BlockSpec(memory_space=pltpu.VMEM)
     scratch = dict(
-        norm=pltpu.VMEM((2, PREFIX, 2048), bf16),
+        norm=pltpu.VMEM((2 * KEYS, 2048), bf16),
+        turn=pltpu.VMEM((32, 128), f32),
+        own_noisy=pltpu.VMEM((128, 128), bf16),
         query_weight=pltpu.VMEM((4, 2, 2, 64, 256), bf16),
         noisy=pltpu.VMEM((8, 128, 128), bf16),
         time=pltpu.VMEM((8, 16, 128), f32),
@@ -611,11 +650,14 @@
         gq=pltpu.VMEM((8, 128, 256), bf16),
         group_gq=pltpu.VMEM((8, 128, 256), bf16),
         wp=pltpu.VMEM((2048, 512), bf16),
-        kv=pltpu.VMEM((2, KEYS, 512), bf16),
-        low=pltpu.VMEM((256, KEYS), bf16),
-        ds=pltpu.VMEM((256, KEYS), bf16),
-        gsum=pltpu.VMEM((512, KEYS), f32),
-        gkv=pltpu.VMEM((2, 512, KEYS), bf16),
+        kv=pltpu.VMEM((2 * KEYS, 512), bf16),
+        low=pltpu.VMEM((512, KEYS), bf16),
+        ds=pltpu.VMEM((512, KEYS), bf16),
+        logits=pltpu.VMEM((256, KEYS), f32),
+        dprob=pltpu.VMEM((256, KEYS), f32),
+        query_t=pltpu.VMEM((8, 256, 64), bf16),
+        cot_t=pltpu.VMEM((8, 256, 64), bf16),
+        gkv=pltpu.VMEM((512, 2 * KEYS), bf16),
         grad=pltpu.VMEM((4, 2, 2, 2, 4, ROWS, 256), f32),
         pair=pltpu.VMEM((4, 4, 4, ROWS, 256), f32),
         grad_query=pltpu.VMEM((4, 2, 2, 64, 256), f32),
@@ -647,7 +689,7 @@
             jax.ShapeDtypeStruct((16, 512), f32),
             jax.ShapeDtypeStruct((8, 512), f32),
         ),
-        in_specs=[smem] * 2 + [pl.BlockSpec(memory_space=pl.ANY)] + [vmem] * 7,
+        in_specs=[smem] * 3 + [pl.BlockSpec(memory_space=pl.ANY)] + [vmem] * 8,
         out_specs=(vmem,) * 4,
         scratch_shapes=[scratch],
         compiler_params=pltpu.CompilerParams(
@@ -658,7 +700,7 @@
         ),
         name="step",
     )(
-        cameras, text_length, hidden, noisy, time, input_weight, cot,
+        cameras, text_length, flow_time, hidden, noise, clean, time, input_weight, cot,
         own_prefix, own_action, own_query,
     )
 
@@ -684,21 +726,17 @@
     query_weight,
     cotangent,
 ):
-    flow_col = flow_time[:, None, None]
-    noisy = (
-        flow_col * action_noise.astype(jnp.float32)
-        + (1.0 - flow_col) * clean_actions.astype(jnp.float32)
-    ).astype(jnp.bfloat16)
-    noisy = jnp.pad(noisy, ((0, 0), (0, PAD_STEPS - STEPS), (0, 96))).reshape(128, 128)
     time = time_feature(flow_time, 1024).reshape(16, 128)
     return step(
         cameras,
         text_length,
+        flow_time,
         prefix_hidden,
-        noisy,
+        action_noise.transpose(0, 2, 1),
+        clean_actions.transpose(0, 2, 1),
         time,
         input_weight,
-        cotangent,
+        cotangent.transpose(1, 0, 2),
         prefix_kv_weight,
         action_kv_weight,
         query_weight,

time: 96.6 us -> 94.6 us (0.979)
  local copies, waits for them, and re-layouts: 9.61 us -> 6.97 us
  Pallas kernels: 83.6 us -> 85.8 us
  other arithmetic: 2.3 us -> 0.82 us
    pallas_call x1, Pallas kernels: 83.6 us -> 85.8 us  [step(): pl.pallas_call(step_kernel, out_shape=(jax.ShapeDtypeStruct((2, STEPS, 20...]
    unnamed x5 -> x3, local copies, waits for them, and re-layouts: 6.18 us -> 4.17 us
where the time goes in v2:
time: 94.6 us; the launch traced here: 94.2 us
  Pallas kernels  85.8 us (91%)
  local copies, waits for them, and re-layouts  6.97 us (7%)
    pallas_call x1, Pallas kernels, step(): pl.pallas_call(step_kernel, out_shape=(jax.ShapeDtypeStruct((2, STEPS, 20...  85.8 us
    unnamed x3, local copies, waits for them, and re-layouts  4.17 us
    pallas_call x1, local copies, waits for them, and re-layouts, step(): pl.pallas_call(step_kernel, out_shape=(jax.ShapeDtypeStruct((2, STEPS, 20...  2.19 us

profile of v2, /device:TPU:0, one launch (start us, length us, event | category | flops | bytes accessed | tf_op | source)
XLA Modules:
  0.0 94.2 jit_solution(11768970762075810449)
XLA Ops:
  0.6 0.8 multiply_sine_fusion
  1.5 0.6 reshape.19.time_ref
  2.1 85.8 %step.1 = (bf16[2,50,2048]{2,1,0:T(8,128)(2,1)}, f32[64,256]{1,0:T(8,128)}, f32[16,512]{1,0:T(8,128)}, f32[8,512]{1,0:T(8,128)}) custom-call(s32[2]{0:T(128)} %cameras_ref.1, s32[2]{0:T(128)} %text_ref.1, f32[2]{0:T(128)} %flow_ref.1, bf16[2,816,2048]{2,1,0:T(8,128)(2,1)} %hidden_ref.1, bf16[2,32,50]{2,1,0:T(8,128)(2,1)} %bitcast.4, ...), custom_call_target="tpu_custom_call" | custom-call | flops 10000000000 | bytes 9000000 | tf_op jit(solution)/shard_map/step/pallas_call | solution.py:684
  87.9 2.2 %copy.15 = bf16[2,50,2048]{2,0,1:T(2,128)(2,1)} copy(bf16[2,50,2048]{2,1,0:T(8,128)(2,1)} %get-tuple-element.4) | data formatting | bytes 819200 | tf_op jit(solution)/shard_map/step/pallas_call | solution.py:684
  90.1 1.5 %copy.19 = f32[64,256]{1,0:T(8,128)} copy(f32[64,256]{1,0:T(8,128)} %get-tuple-element.15) | data formatting | bytes 131072
  91.5 1.4 %copy.20 = f32[16,512]{1,0:T(8,128)} copy(f32[16,512]{1,0:T(8,128)} %get-tuple-element.16) | data formatting | bytes 65536
  92.9 1.3 %copy.21 = f32[8,512]{1,0:T(8,128)} copy(f32[8,512]{1,0:T(8,128)} %get-tuple-element.17) | data formatting | bytes 32768
  (2 shorter events, 0.0 us)

commit v3 on v2

--- a/solution.py
+++ b/solution.py
@@ -10,7 +10,7 @@
 IMG = 256
 EPS = 1e-06
 MESH = pl.DeviceIdType.MESH
-VMEM_LIMIT = 58 * 1024 * 1024
+VMEM_LIMIT = 50 * 1024 * 1024
 PREFIX, STEPS, PAD_STEPS, KEYS = 816, 50, 64, 896
 
 ROWS = 48
@@ -46,8 +46,8 @@
         return lax.rem(self.at[axis] + by, 4)
 
     def group_member(self, offset, sign=1):
-        z_lo = lax.rem(self.z_lo + offset // 4, 2)
-        x = lax.rem(self.at["x"] + sign * (offset % 4) + 4, 4)
+        z_lo = lax.rem(self.z_lo + lax.div(offset, 4), 2)
+        x = lax.rem(self.at["x"] + sign * lax.rem(offset, 4) + 4, 4)
         return z_lo * 4 + x
 
     def greet(self):
@@ -59,7 +59,10 @@
         others.append(self.device(z=beyond))
         for other in others:
             pl.semaphore_signal(barrier, inc=1, device_id=other, device_id_type=MESH)
-        pl.semaphore_wait(barrier, len(others))
+        self.greeted = len(others)
+
+    def meet(self):
+        pl.semaphore_wait(pltpu.get_barrier_semaphore(), self.greeted)
 
 
 class Links:
@@ -296,18 +299,12 @@
     )
 
 
-def rows_dot(left, right):
-    return lax.dot_general(
-        left, right, (((0,), (0,)), ((), ())), preferred_element_type=jnp.float32
-    )
-
-
 def dot(left, right):
     return jnp.dot(left, right, preferred_element_type=jnp.float32)
 
 
 def step_kernel(
-    cameras_ref, text_ref, flow_ref, hidden_ref, noise_ref, clean_ref, time_ref, input_ref, cot_ref,
+    cameras_ref, text_ref, flow_ref, hidden_ref, noise_ref, clean_ref, sin_ref, cos_ref, input_ref, cot_ref,
     own_prefix_ref, own_action_ref, own_query_ref,
     attended_ref, out_query_ref, out_prefix_ref, out_action_ref,
     v,
@@ -317,6 +314,7 @@
     core, y, z_hi, z_lo, x = place.core, place.at["y"], place.z_hi, place.z_lo, place.at["x"]
     seq = place.seq
     links = Links(v["send"], v["recv"])
+    place.greet()
 
     norm = v["norm"]
     loads = []
@@ -348,55 +346,65 @@
             turn[...].T[0:PAD_STEPS].astype(bf16)
         )
     v["noisy"][seq] = own_noisy[...]
-    v["time"][seq] = time_ref[...]
-    place.greet()
+    own_time = v["own_time"]
+    own_time[:, 0:512] = sin_ref[...]
+    own_time[:, 512:1024] = cos_ref[...]
+    v["time"][seq] = own_time[...]
+    place.meet()
+
+    eye = v["eye"]
+    row = lax.broadcasted_iota(jnp.int32, (256, 256), 0)
+    col = lax.broadcasted_iota(jnp.int32, (256, 256), 1)
+    eye[...] = jnp.where(row == col, 1.0, 0.0).astype(bf16)
 
     packet = links.slots(16)
     for offset in range(1, 8):
         to = (place.dp, place.group_member(offset))
         links.go(own_noisy, v["noisy"].at[seq], to, packet + offset)
-        links.go(time_ref, v["time"].at[seq], to, packet + 8 + offset)
+        links.go(own_time, v["time"].at[seq], to, packet + 8 + offset)
 
     act, act_t = v["act"], v["act_t"]
 
-    def action_rows(offset):
+    def make_rows(member):
+        at = pl.ds(pl.multiple_of(member * 128, 128), 128)
+        wide = dot(v["noisy"][member][:, 0:32], input_ref[...])
+        time = v["time"][member]
+        parts = []
+        for s in range(2):
+            part = wide[s * PAD_STEPS : (s + 1) * PAD_STEPS] + time[s : s + 1]
+            scale = lax.rsqrt(jnp.mean(part * part, axis=-1, keepdims=True) + EPS)
+            parts.append((part * scale).astype(bf16))
+        rows = jnp.concatenate(parts, axis=0)
+        act[at, :] = rows
+        for f in range(4):
+            cols = slice(f * 256, (f + 1) * 256)
+            act_t[cols, at] = lanes_dot(eye[...], rows[:, cols]).astype(bf16)
+
+    def spread_rows():
+        at = pl.ds(pl.multiple_of(seq * 128, 128), 128)
+        feature = lax.broadcasted_iota(jnp.int32, (256, 128), 1)
+        k = lax.broadcasted_iota(jnp.int32, (256, 128), 0)
+        within = k % 16
+        origin = (k // 16) * 8 + within
+        first = jnp.where((within < 8) & (feature == origin), 1.0, 0.0).astype(bf16)
+        second = jnp.where((within >= 8) & (feature == origin - 8), 1.0, 0.0).astype(bf16)
+        for spread, name in ((first, "left"), (second, "right")):
+            for i in range(8):
+                cols, wide = slice(i * 128, (i + 1) * 128), slice(i * 256, (i + 1) * 256)
+                v[name][:, wide] = lanes_dot(act[at, cols], spread).astype(bf16)
+                v[name + "_t"][wide, :] = dot(spread, act_t[cols, at]).astype(bf16)
+
+    def group_rows(low, high):
         def run():
-            member = place.group_member(offset, -1)
-            if offset:
+            members = [place.group_member(offset, -1) for offset in range(low, high)]
+            for offset, member in zip(range(low, high), members):
+                if offset == 0:
+                    continue
                 to = (place.dp, member)
                 links.arrived(v["noisy"].at[member], to, packet + offset)
                 links.arrived(v["time"].at[member], to, packet + 8 + offset)
-            wide = dot(v["noisy"][member][:, 0:32], input_ref[...])
-            time = v["time"][member]
-            pieces = []
-            for s in range(2):
-                rows = slice(s * PAD_STEPS, (s + 1) * PAD_STEPS)
-                pieces.append(
-                    jnp.concatenate(
-                        [
-                            wide[rows, i * 128 : (i + 1) * 128] + time[s * 8 + i : s * 8 + i + 1]
-                            for i in range(8)
-                        ],
-                        axis=1,
-                    )
-                )
-            wide = jnp.concatenate(pieces, axis=0)
-            scale = lax.rsqrt(jnp.mean(wide * wide, axis=-1, keepdims=True) + EPS)
-            rows = (wide * scale).astype(bf16)
-            at = pl.ds(pl.multiple_of(member * 128, 128), 128)
-            act[at, :] = rows
-            act_t[:, at] = rows.T
-            if offset == 0:
-                row = lax.broadcasted_iota(jnp.int32, (128, 256), 0)
-                col = lax.broadcasted_iota(jnp.int32, (128, 256), 1)
-                within = col % 16
-                origin = (col // 16) * 8 + within
-                to_left = jnp.where((within < 8) & (row == origin), 1.0, 0.0).astype(bf16)
-                to_right = jnp.where((within >= 8) & (row == origin - 8), 1.0, 0.0).astype(bf16)
-                for i in range(8):
-                    piece, cols = rows[:, i * 128 : (i + 1) * 128], slice(i * 256, (i + 1) * 256)
-                    v["left"][:, cols] = dot(piece, to_left).astype(bf16)
-                    v["right"][:, cols] = dot(piece, to_right).astype(bf16)
+            for member in members:
+                make_rows(member)
 
         return run
 
@@ -405,55 +413,59 @@
             loads[chunk].wait()
             s, start, count = chunks[chunk]
 
-            def body(i, carry):
-                places = [
+            def places(i):
+                return [
                     pl.ds(pl.multiple_of(s * KEYS + start + i * 48 + j * 16, 16), 16)
                     for j in range(3)
                 ]
-                scales = []
-                for at in places:
+
+            def scales(i):
+                found = []
+                for at in places(i):
                     wide = norm[at, :].astype(f32)
-                    scales.append(lax.rsqrt(jnp.mean(wide * wide, axis=-1, keepdims=True) + EPS))
-                for at, scale in zip(places, scales):
+                    found.append(lax.rsqrt(jnp.mean(wide * wide, axis=-1, keepdims=True) + EPS))
+                return tuple(found)
+
+            def body(i, present):
+                following = scales(jnp.minimum(i + 1, count // 48 - 1))
+                for at, scale in zip(places(i), present):
                     norm[at, :] = (norm[at, :].astype(f32) * scale).astype(bf16)
-                return carry
-
-            lax.fori_loop(0, count // 48, body, 0)
+                return following
+
+            lax.fori_loop(0, count // 48, body, scales(0))
 
         return run
 
-    def place_cotangent():
+    def place_rows():
         v["cot"][...] = jnp.zeros_like(v["cot"])
-        for s in range(2):
-            norm[s * KEYS + PREFIX : (s + 1) * KEYS, :] = jnp.zeros((KEYS - PREFIX, 2048), bf16)
         for s in range(2):
             for h in range(8):
                 v["cot"][h, s * PAD_STEPS : s * PAD_STEPS + STEPS, :] = cot_ref[
                     :, s, h * 256 : (h + 1) * 256
                 ]
+        for s in range(2):
+            norm[s * KEYS + PREFIX : (s + 1) * KEYS, :] = jnp.zeros((KEYS - PREFIX, 2048), bf16)
 
     exchange = links.slots(16)
 
     def send_queries():
         wide = query_weight[...].reshape(1024, 256)
-        for offset in (1, 2, 3, 4, 5, 6, 7, 0):
+        for half in range(2):
+            rows = slice(half * 512, (half + 1) * 512)
+            value = dot(act[rows, :], wide).astype(bf16)
+            v["query_out"][half * 4 : half * 4 + 4] = value.reshape(4, 128, 256)
+        for offset in range(1, 8):
             member = place.group_member(offset)
-            at = pl.ds(pl.multiple_of(member * 128, 128), 128)
-            value = dot(act[at, :], wide).astype(bf16)
-            if offset:
-                v["query_out"][offset] = value
-                links.go(
-                    v["query_out"].at[offset], v["query"].at[seq], (place.dp, member),
-                    exchange + offset,
-                )
-            else:
-                v["query"][seq] = value
+            links.go(
+                v["query_out"].at[member], v["query"].at[seq], (place.dp, member),
+                exchange + offset,
+            )
+        v["query"][seq] = v["query_out"][seq]
 
     works = [gather_query(links, place, query_weight, send_queries)]
     works += [gather_part(links, place, v[f"weight_{part}"], ORDERS[part]) for part in range(3)]
-    rows = [action_rows(offset) for offset in range(8)]
-    tasks = [rows[0], lambda: [rows[i]() for i in (1, 3, 4)], lambda: [rows[i]() for i in (2, 5, 6, 7)]]
-    tasks += [normalize(chunk) for chunk in range(6)] + [place_cotangent]
+    tasks = [normalize(0), normalize(1), group_rows(0, 4), group_rows(4, 8)]
+    tasks += [normalize(chunk) for chunk in range(2, 6)] + [spread_rows, place_rows]
     run_together(works, tasks)
 
     wp, kv = v["wp"], v["kv"]
@@ -490,11 +502,11 @@
     keys, values = keys.astype(bf16), values.astype(bf16)
 
     def prefix(i, carry):
-        at = pl.ds(pl.multiple_of(i * 256, 256), 256)
+        at = pl.ds(pl.multiple_of(i * 448, 64), 448)
         kv[at, :] = dot(norm[at, :], wp[...]).astype(bf16)
         return carry
 
-    lax.fori_loop(0, 7, prefix, 0)
+    lax.fori_loop(0, 4, prefix, 0)
     for s in range(2):
         rows = slice(s * PAD_STEPS, (s + 1) * PAD_STEPS)
         start = s * KEYS + PREFIX
@@ -506,7 +518,6 @@
         links.arrived(v["query"].at[member], (place.dp, member), exchange + offset)
 
     low_ref, ds_ref, gkv = v["low"], v["ds"], v["gkv"]
-    logits_ref, dprob_ref = v["logits"], v["dprob"]
 
     def sixteenth(rows):
         return (rows.astype(f32) * 0.0625).astype(bf16)
@@ -519,49 +530,44 @@
         column = lax.broadcasted_iota(jnp.int32, (1, KEYS), 1)
         valid = (column < length) | ((column >= PREFIX) & (column < PREFIX + STEPS))
         bias = jnp.where(valid, 0.0, -1e30)
-        for i in range(2):
-            heads = slice(i * 4, i * 4 + 4)
-            half = slice(i * 256, (i + 1) * 256)
-            query = v["query"][heads, mine, :].reshape(256, 256)
-            cot = v["cot"][heads, mine, :].reshape(256, 256)
-            logits_ref[...] = lanes_dot(sixteenth(query), kv[tokens, 0:256])
-            dprob_ref[...] = lanes_dot(sixteenth(cot), kv[tokens, 256:512])
-
-            def softmax(b, carry):
-                at = pl.ds(pl.multiple_of(b * 16, 16), 16)
-                to = pl.ds(pl.multiple_of(i * 256 + b * 16, 16), 16)
-                logits = logits_ref[at, :] + bias
-                expo = jnp.exp(logits - jnp.max(logits, axis=-1, keepdims=True))
-                probs = expo * (1.0 / jnp.sum(expo, axis=-1, keepdims=True))
-                low_ref[to, :] = probs.astype(bf16)
-                dprob = dprob_ref[at, :]
-                inner = jnp.sum(probs * dprob, axis=-1, keepdims=True)
-                ds_ref[to, :] = (probs * (dprob - inner)).astype(bf16)
-                return carry
-
-            lax.fori_loop(0, 16, softmax, 0, unroll=4)
-            attended = dot(low_ref[half, :], kv[tokens, 256:512]).astype(bf16)
-            for j in range(4):
-                at = slice((i * 4 + j) * 256, (i * 4 + j + 1) * 256)
-                attended_ref[s, :, at] = attended[j * 64 : j * 64 + STEPS]
-            grad = dot(ds_ref[half, :], kv[tokens, 0:256]).astype(bf16)
-            v["gq"][heads, mine, :] = grad.reshape(4, 64, 256)
+        query = v["query"][:, mine, :].reshape(512, 256)
+        cot = v["cot"][:, mine, :].reshape(512, 256)
+        logits = lanes_dot(sixteenth(query), kv[tokens, 0:256]) + bias
+        expo = jnp.exp(logits - jnp.max(logits, axis=-1, keepdims=True))
+        probs = expo * (1.0 / jnp.sum(expo, axis=-1, keepdims=True))
+        low_ref[...] = probs.astype(bf16)
+        dprob = lanes_dot(sixteenth(cot), kv[tokens, 256:512])
+        inner = jnp.sum(probs * dprob, axis=-1, keepdims=True)
+        ds_ref[...] = (probs * (dprob - inner)).astype(bf16)
+        v["gq"][:, mine, :] = dot(ds_ref[...], kv[tokens, 0:256]).astype(bf16).reshape(8, 64, 256)
+        attended = dot(low_ref[...], kv[tokens, 256:512]).astype(bf16)
         for h in range(8):
-            v["query_t"][h] = v["query"][h, mine, :].T
-            v["cot_t"][h] = v["cot"][h, mine, :].T
-
-        def tile(t, carry):
-            at = pl.ds(pl.multiple_of(t * 128, 128), 128)
-            to = pl.ds(pl.multiple_of(s * KEYS + t * 128, 128), 128)
+            attended_ref[s, :, h * 256 : (h + 1) * 256] = attended[h * 64 : h * 64 + STEPS]
+
+        first = lax.broadcasted_iota(jnp.int32, (256, 128), 1) < 64
+        for rows, turned in ((query, v["query_t"]), (cot, v["cot_t"])):
+            across = lanes_dot(eye[...], rows)
+            for h in range(8):
+                pair = across[:, (h // 2) * 128 : (h // 2 + 1) * 128]
+                keep = first if h % 2 == 0 else jnp.logical_not(first)
+                turned[h] = jnp.where(keep, pair, 0.0).astype(bf16)
+
+        def tile(begin, width):
+            at = pl.ds(begin, width)
+            to = pl.ds(pl.multiple_of(start + begin, 128), width)
             for left, right, top in ((v["query_t"], ds_ref, 0), (v["cot_t"], low_ref, 256)):
-                total = jnp.zeros((256, 128), f32)
+                total = jnp.zeros((256, width), f32)
                 for h in range(8):
-                    term = dot(left[h], right[h * 64 : (h + 1) * 64, at])
+                    term = dot(left[h], right[(h // 2) * 128 : (h // 2 + 1) * 128, at])
                     total = total + term.astype(bf16).astype(f32)
                 gkv[top : top + 256, to] = total.astype(bf16)
+
+        def wide_tile(t, carry):
+            tile(pl.multiple_of(t * 256, 256), 256)
             return carry
 
-        lax.fori_loop(0, 7, tile, 0)
+        lax.fori_loop(0, 3, wide_tile, 0)
+        tile(768, 128)
         return carry
 
     lax.fori_loop(0, 2, sample, 0)
@@ -589,19 +595,18 @@
         at = pl.ds(pl.multiple_of(k * 256, 256), 256)
         a, b = k // 2, lax.rem(k, 2)
         value = dot(gkv[...], norm[:, at])
-        value = value.T
+        high = value.astype(bf16)
+        low = (value - high.astype(f32)).astype(bf16)
+        value = lanes_dot(eye[...], high) + lanes_dot(eye[...], low)
         grad[a, b, :, :, :, 0:16, :] = value[:, 0:256].reshape(2, 2, 4, 16, 256)
         grad[a, b, :, :, :, 16:32, :] = value[:, 256:512].reshape(2, 2, 4, 16, 256)
-        action = rows_dot(v["left"][:, at], ds_ref[0:128, 0:256])
-        action += rows_dot(v["right"][:, at], ds_ref[0:128, 256:512])
+        action = dot(v["left_t"][at, :], ds_ref[0:128, 0:256])
+        action += dot(v["right_t"][at, :], ds_ref[0:128, 256:512])
         grad[a, b, :, :, :, 32:48, :] = action.reshape(2, 2, 4, 16, 256)
         pair_op(k).start()
         return carry
 
-    lax.fori_loop(0, 8, grad_prefix, 0)
-    for k in range(8):
-        pair_op(k).wait_recv()
-
+    lax.fori_loop(0, 8, grad_prefix, 0, unroll=2)
     def grad_query():
         for offset in range(1, 8):
             member = place.group_member(offset, -1)
@@ -621,16 +626,31 @@
 
         return store
 
-    works = [reduce_part(links, place, grad, pair, v, part, finish(part)) for part in range(3)]
-    works.append(reduce_query(links, place, grad_query, v, out_query_ref))
-    run_together(works)
+    def paired():
+        for k in range(8):
+            pair_op(k).wait_recv()
+        yield
+
+    works = [reduce_query(links, place, grad_query, v, out_query_ref), paired()]
+    works += [reduce_part(links, place, grad, pair, v, part, finish(part)) for part in range(3)]
+    early = list(links.sent)
+    links.sent.clear()
+
+    def drain(ops):
+        def run():
+            for op in ops:
+                op.wait_send()
+
+        return run
+
+    run_together(works, [drain(early[i::4]) for i in range(4)])
     for op in links.sent:
         op.wait_send()
     for k in range(8):
         pair_op(k).wait_send()
 
 
-def step(cameras, text_length, flow_time, hidden, noise, clean, time, input_weight, cot, own_prefix, own_action, own_query):
+def step(cameras, text_length, flow_time, hidden, noise, clean, sine, cosine, input_weight, cot, own_prefix, own_action, own_query):
     bf16, f32 = jnp.bfloat16, jnp.float32
     smem, vmem = pl.BlockSpec(memory_space=pltpu.SMEM), pl.BlockSpec(memory_space=pltpu.VMEM)
     scratch = dict(
@@ -639,12 +659,16 @@
         own_noisy=pltpu.VMEM((128, 128), bf16),
         query_weight=pltpu.VMEM((4, 2, 2, 64, 256), bf16),
         noisy=pltpu.VMEM((8, 128, 128), bf16),
-        time=pltpu.VMEM((8, 16, 128), f32),
+        time=pltpu.VMEM((8, 2, 1024), f32),
+        own_time=pltpu.VMEM((2, 1024), f32),
         act=pltpu.VMEM((1024, 1024), bf16),
         act_t=pltpu.VMEM((1024, 1024), bf16),
         left=pltpu.VMEM((128, 2048), bf16),
         right=pltpu.VMEM((128, 2048), bf16),
         cot=pltpu.VMEM((8, 128, 256), bf16),
+        eye=pltpu.VMEM((256, 256), bf16),
+        left_t=pltpu.VMEM((2048, 128), bf16),
+        right_t=pltpu.VMEM((2048, 128), bf16),
         query=pltpu.VMEM((8, 128, 256), bf16),
         query_out=pltpu.VMEM((8, 128, 256), bf16),
         gq=pltpu.VMEM((8, 128, 256), bf16),
@@ -653,10 +677,8 @@
         kv=pltpu.VMEM((2 * KEYS, 512), bf16),
         low=pltpu.VMEM((512, KEYS), bf16),
         ds=pltpu.VMEM((512, KEYS), bf16),
-        logits=pltpu.VMEM((256, KEYS), f32),
-        dprob=pltpu.VMEM((256, KEYS), f32),
-        query_t=pltpu.VMEM((8, 256, 64), bf16),
-        cot_t=pltpu.VMEM((8, 256, 64), bf16),
+        query_t=pltpu.VMEM((8, 256, 128), bf16),
+        cot_t=pltpu.VMEM((8, 256, 128), bf16),
         gkv=pltpu.VMEM((512, 2 * KEYS), bf16),
         grad=pltpu.VMEM((4, 2, 2, 2, 4, ROWS, 256), f32),
         pair=pltpu.VMEM((4, 4, 4, ROWS, 256), f32),
@@ -689,7 +711,7 @@
             jax.ShapeDtypeStruct((16, 512), f32),
             jax.ShapeDtypeStruct((8, 512), f32),
         ),
-        in_specs=[smem] * 3 + [pl.BlockSpec(memory_space=pl.ANY)] + [vmem] * 8,
+        in_specs=[smem] * 3 + [pl.BlockSpec(memory_space=pl.ANY)] + [vmem] * 9,
         out_specs=(vmem,) * 4,
         scratch_shapes=[scratch],
         compiler_params=pltpu.CompilerParams(
@@ -700,7 +722,7 @@
         ),
         name="step",
     )(
-        cameras, text_length, flow_time, hidden, noise, clean, time, input_weight, cot,
+        cameras, text_length, flow_time, hidden, noise, clean, sine, cosine, input_weight, cot,
         own_prefix, own_action, own_query,
     )
 
@@ -710,7 +732,7 @@
     fraction = jnp.arange(half_width, dtype=jnp.float32) / (half_width - 1)
     period = 0.004 * 1000.0**fraction
     angle = flow_col[..., None] * (2.0 * math.pi / period)
-    return jnp.concatenate([jnp.sin(angle), jnp.cos(angle)], axis=-1)
+    return jnp.sin(angle), jnp.cos(angle)
 
 
 def on_device(
@@ -726,7 +748,7 @@
     query_weight,
     cotangent,
 ):
-    time = time_feature(flow_time, 1024).reshape(16, 128)
+    sine, cosine = time_feature(flow_time, 1024)
     return step(
         cameras,
         text_length,
@@ -734,7 +756,8 @@
         prefix_hidden,
         action_noise.transpose(0, 2, 1),
         clean_actions.transpose(0, 2, 1),
-        time,
+        sine,
+        cosine,
         input_weight,
         cotangent.transpose(1, 0, 2),
         prefix_kv_weight,

time: 94.6 us -> 97.3 us (1.029)
  local copies, waits for them, and re-layouts: 6.97 us -> 10.4 us
    unnamed x3 -> x23, local copies, waits for them, and re-layouts: 4.17 us -> 9.25 us
    pallas_call x1, local copies, waits for them, and re-layouts: 2.19 us -> 1.17 us  [step(): pl.pallas_call(step_kernel, out_shape=(jax.ShapeDtypeStruct((2, STEPS, 20...]
where the time goes in v3:
time: 97.3 us; the launch traced here: 96.8 us
  Pallas kernels  84.9 us (87%)
  local copies, waits for them, and re-layouts  10.4 us (11%)
    pallas_call x1, Pallas kernels, step(): pl.pallas_call(step_kernel, out_shape=(jax.ShapeDtypeStruct((2, STEPS, 20...  84.9 us
    unnamed x23, local copies, waits for them, and re-layouts  9.25 us

profile of v3, /device:TPU:0, one launch (start us, length us, event | category | flops | bytes accessed | tf_op | source)
XLA Modules:
  0.0 96.8 jit_solution(18228142231705835488)
XLA Ops:
  0.6 0.8 multiply_cosine_fusion
  1.4 0.0 copy-start
  1.5 0.6 copy-done
  2.1 0.0 copy-start.1
  2.1 1.0 %copy-done.1 = bf16[2,50,2048]{2,0,1:T(2,128)(2,1)S(1)} copy-done((bf16[2,50,2048]{2,0,1:T(2,128)(2,1)S(1)}, bf16[2,50,2048]{2,0,1:T(2,128)(2,1)}, u32[]{:S(2)}) %copy-start.1) | copy-done | bytes 409624
  3.1 0.0 copy-start.2
  3.1 0.8 copy-done.2
  4.0 0.0 copy-start.3
  4.0 0.8 copy-done.3
  4.7 0.0 copy-start.4
  4.7 0.7 copy-done.4
  5.4 0.0 copy-start.5
  5.4 0.7 copy-done.5
  6.1 0.0 copy-start.6
  6.1 0.7 copy-done.6
  6.9 0.0 copy-start.7
  6.9 0.7 copy-done.7
  7.6 0.0 copy-start.8
  7.6 0.7 copy-done.8
  8.2 0.0 copy-start.9
  8.2 0.7 copy-done.9
  8.9 84.9 %step.1 = (bf16[2,50,2048]{2,1,0:T(8,128)(2,1)S(1)}, f32[64,256]{1,0:T(8,128)S(1)}, f32[16,512]{1,0:T(8,128)S(1)}, f32[8,512]{1,0:T(8,128)S(1)}) custom-call(s32[2]{0:T(128)S(1)} %copy-done.8, s32[2]{0:T(128)S(1)} %copy-done.9, f32[2]{0:T(128)S(1)} %copy-done, bf16[2,816,2048]{2,1,0:T(8,128)(2,1)} %hidden_ref.1, bf16[2,32,50]{2,1,0:T(8,128)(2,1)S(1)} %bitcast.4, ...), custom_call_target="tpu_custom_call" | custom-call | flops 10000000000 | bytes 9000000 | tf_op jit(solution)/shard_map/step/pallas_call | solution.py:706
  93.8 1.2 %copy.15 = bf16[2,50,2048]{2,0,1:T(2,128)(2,1)} copy(bf16[2,50,2048]{2,1,0:T(8,128)(2,1)S(1)} %get-tuple-element.4) | data formatting | bytes 819200 | tf_op jit(solution)/shard_map/step/pallas_call | solution.py:706
  94.9 0.6 copy.19
  95.6 0.6 copy.20
  96.2 0.6 copy.21
  (1 shorter events, 0.0 us)
Async XLA Ops:
  1.4 0.7 copy-start
  2.1 1.0 %copy-start.1 = (bf16[2,50,2048]{2,0,1:T(2,128)(2,1)S(1)}, bf16[2,50,2048]{2,0,1:T(2,128)(2,1)}, u32[]{:S(2)}) copy-start(bf16[2,50,2048]{2,0,1:T(2,128)(2,1)} %param.21) | copy-start | bytes 1228804
  3.1 0.8 copy-start.2
  4.0 0.8 copy-start.3
  4.7 0.7 copy-start.4
  5.4 0.7 copy-start.5
  6.1 0.7 copy-start.6
  6.9 0.7 copy-start.7
  7.6 0.7 copy-start.8
  8.2 0.7 copy-start.9

commit v4 on v3

--- a/solution.py
+++ b/solution.py
@@ -287,10 +287,11 @@
     own = place.at["y"]
     value = grad_ref[own, :, core] + pair_ref[own]
     total[...] = value + full[0].astype(f32) + full[1].astype(f32)
-    links.go(total.at[1 - z_hi], far_ref, place.z_far, slot + 7)
+    v["query_far_out"][...] = total[1 - z_hi].astype(bf16)
+    links.go(v["query_far_out"], far_ref, place.z_far, slot + 7)
     yield
     links.arrived(far_ref, place.z_far, slot + 7)
-    out_ref[...] = total[z_hi] + far_ref[...]
+    out_ref[...] = total[z_hi] + far_ref[...].astype(f32)
 
 
 def lanes_dot(left, right):
@@ -299,13 +300,19 @@
     )
 
 
+def rows_dot(left, right):
+    return lax.dot_general(
+        left, right, (((0,), (0,)), ((), ())), preferred_element_type=jnp.float32
+    )
+
+
 def dot(left, right):
     return jnp.dot(left, right, preferred_element_type=jnp.float32)
 
 
 def step_kernel(
-    cameras_ref, text_ref, flow_ref, hidden_ref, noise_ref, clean_ref, sin_ref, cos_ref, input_ref, cot_ref,
-    own_prefix_ref, own_action_ref, own_query_ref,
+    cameras_hbm, text_hbm, flow_hbm, hidden_hbm, noise_hbm, clean_hbm, input_hbm, cot_hbm,
+    own_prefix_hbm, own_action_hbm, own_query_hbm, sin_ref, cos_ref,
     attended_ref, out_query_ref, out_prefix_ref, out_action_ref,
     v,
 ):
@@ -317,11 +324,20 @@
     place.greet()
 
     norm = v["norm"]
+    operands = dict(
+        flow=flow_hbm, noise=noise_hbm, clean=clean_hbm, own_prefix=own_prefix_hbm,
+        own_action=own_action_hbm, own_query=own_query_hbm, input=input_hbm, cot_in=cot_hbm,
+        cameras=cameras_hbm, text=text_hbm,
+    )
+    fetches = {}
+    for i, (name, ref) in enumerate(operands.items()):
+        fetches[name] = pltpu.make_async_copy(ref, v[name], v["load"].at[6 + i])
+        fetches[name].start()
     loads = []
     chunks = [(s, start, count) for s in range(2) for start, count in ((0, 288), (288, 288), (576, 240))]
     for k, (s, start, count) in enumerate(chunks):
         load = pltpu.make_async_copy(
-            hidden_ref.at[s, pl.ds(start, count), :],
+            hidden_hbm.at[s, pl.ds(start, count), :],
             norm.at[pl.ds(s * KEYS + start, count), :],
             v["load"].at[k],
         )
@@ -329,22 +345,23 @@
         loads.append(load)
 
     query_weight = v["query_weight"]
-    own_action = own_action_ref[...].astype(f32)
+    for name in ("flow", "noise", "clean", "own_prefix", "own_action", "own_query"):
+        fetches[name].wait()
+    own_prefix = v["own_prefix"]
+    own_action = v["own_action"][...].astype(f32)
     own_action = jnp.concatenate([own_action[:, 0:256], own_action[:, 256:512]], axis=0)
-    own_parts = (own_prefix_ref[:, 0:256], own_prefix_ref[:, 256:512], own_action.astype(bf16))
+    own_parts = (own_prefix[:, 0:256], own_prefix[:, 256:512], own_action.astype(bf16))
     for part, (first, second, third) in enumerate(ORDERS):
         at = place.at
         v[f"weight_{part}"][core, at[third], at[second], at[first]] = own_parts[part]
-    query_weight[y, z_hi, core] = own_query_ref[...]
-    turn, own_noisy = v["turn"], v["own_noisy"]
-    turn[...] = jnp.zeros_like(turn)
-    own_noisy[...] = jnp.zeros_like(own_noisy)
+    query_weight[y, z_hi, core] = v["own_query"][...]
+    own_noisy = v["own_noisy"]
+    noisy = []
     for s in range(2):
-        t = flow_ref[s]
-        turn[:, 0:STEPS] = t * noise_ref[s].astype(f32) + (1.0 - t) * clean_ref[s].astype(f32)
-        own_noisy[s * PAD_STEPS : (s + 1) * PAD_STEPS, 0:32] = (
-            turn[...].T[0:PAD_STEPS].astype(bf16)
-        )
+        t = v["flow"][s]
+        noisy.append(t * v["noise"][s].astype(f32) + (1.0 - t) * v["clean"][s].astype(f32))
+    blank = jnp.zeros((32, PAD_STEPS - STEPS), f32)
+    own_noisy[...] = jnp.concatenate([noisy[0], blank, noisy[1], blank], axis=1).astype(bf16)
     v["noisy"][seq] = own_noisy[...]
     own_time = v["own_time"]
     own_time[:, 0:512] = sin_ref[...]
@@ -358,16 +375,18 @@
     eye[...] = jnp.where(row == col, 1.0, 0.0).astype(bf16)
 
     packet = links.slots(16)
-    for offset in range(1, 8):
-        to = (place.dp, place.group_member(offset))
-        links.go(own_noisy, v["noisy"].at[seq], to, packet + offset)
-        links.go(own_time, v["time"].at[seq], to, packet + 8 + offset)
+    def send_packets():
+        for offset in range(1, 8):
+            to = (place.dp, place.group_member(offset))
+            links.go(own_noisy, v["noisy"].at[seq], to, packet + offset)
+            links.go(own_time, v["time"].at[seq], to, packet + 8 + offset)
+        fetches["input"].wait()
 
     act, act_t = v["act"], v["act_t"]
 
     def make_rows(member):
         at = pl.ds(pl.multiple_of(member * 128, 128), 128)
-        wide = dot(v["noisy"][member][:, 0:32], input_ref[...])
+        wide = rows_dot(v["noisy"][member], v["input"][...])
         time = v["time"][member]
         parts = []
         for s in range(2):
@@ -437,10 +456,11 @@
         return run
 
     def place_rows():
+        fetches["cot_in"].wait()
         v["cot"][...] = jnp.zeros_like(v["cot"])
         for s in range(2):
             for h in range(8):
-                v["cot"][h, s * PAD_STEPS : s * PAD_STEPS + STEPS, :] = cot_ref[
+                v["cot"][h, s * PAD_STEPS : s * PAD_STEPS + STEPS, :] = v["cot_in"][
                     :, s, h * 256 : (h + 1) * 256
                 ]
         for s in range(2):
@@ -464,7 +484,7 @@
 
     works = [gather_query(links, place, query_weight, send_queries)]
     works += [gather_part(links, place, v[f"weight_{part}"], ORDERS[part]) for part in range(3)]
-    tasks = [normalize(0), normalize(1), group_rows(0, 4), group_rows(4, 8)]
+    tasks = [lambda: (send_packets(), normalize(0)()), normalize(1), group_rows(0, 4), group_rows(4, 8)]
     tasks += [normalize(chunk) for chunk in range(2, 6)] + [spread_rows, place_rows]
     run_together(works, tasks)
 
@@ -517,13 +537,15 @@
         member = place.group_member(offset, -1)
         links.arrived(v["query"].at[member], (place.dp, member), exchange + offset)
 
+    fetches["cameras"].wait()
+    fetches["text"].wait()
     low_ref, ds_ref, gkv = v["low"], v["ds"], v["gkv"]
 
     def sixteenth(rows):
         return (rows.astype(f32) * 0.0625).astype(bf16)
 
     def sample(s, carry):
-        length = cameras_ref[s] * IMG + text_ref[s]
+        length = v["cameras"][s] * IMG + v["text"][s]
         mine = pl.ds(pl.multiple_of(s * PAD_STEPS, PAD_STEPS), PAD_STEPS)
         start = pl.multiple_of(s * KEYS, 128)
         tokens = pl.ds(start, KEYS)
@@ -650,15 +672,17 @@
         pair_op(k).wait_send()
 
 
-def step(cameras, text_length, flow_time, hidden, noise, clean, sine, cosine, input_weight, cot, own_prefix, own_action, own_query):
+def step(
+    cameras, text_length, flow_time, hidden, noise, clean, input_weight, cot,
+    own_prefix, own_action, own_query, sine, cosine,
+):
     bf16, f32 = jnp.bfloat16, jnp.float32
-    smem, vmem = pl.BlockSpec(memory_space=pltpu.SMEM), pl.BlockSpec(memory_space=pltpu.VMEM)
+    hbm, vmem = pl.BlockSpec(memory_space=pltpu.HBM), pl.BlockSpec(memory_space=pltpu.VMEM)
     scratch = dict(
         norm=pltpu.VMEM((2 * KEYS, 2048), bf16),
-        turn=pltpu.VMEM((32, 128), f32),
-        own_noisy=pltpu.VMEM((128, 128), bf16),
+        own_noisy=pltpu.VMEM((32, 128), bf16),
         query_weight=pltpu.VMEM((4, 2, 2, 64, 256), bf16),
-        noisy=pltpu.VMEM((8, 128, 128), bf16),
+        noisy=pltpu.VMEM((8, 32, 128), bf16),
         time=pltpu.VMEM((8, 2, 1024), f32),
         own_time=pltpu.VMEM((2, 1024), f32),
         act=pltpu.VMEM((1024, 1024), bf16),
@@ -688,10 +712,21 @@
         query_half=pltpu.VMEM((2, 64, 256), bf16),
         query_full=pltpu.VMEM((2, 2, 64, 256), bf16),
         query_sum=pltpu.VMEM((2, 64, 256), f32),
-        query_far=pltpu.VMEM((64, 256), f32),
+        query_far=pltpu.VMEM((64, 256), bf16),
+        query_far_out=pltpu.VMEM((64, 256), bf16),
         send=pltpu.SemaphoreType.DMA((192,)),
         recv=pltpu.SemaphoreType.DMA((192,)),
-        load=pltpu.SemaphoreType.DMA((6,)),
+        load=pltpu.SemaphoreType.DMA((16,)),
+        flow=pltpu.SMEM((2,), f32),
+        cameras=pltpu.SMEM((2,), jnp.int32),
+        text=pltpu.SMEM((2,), jnp.int32),
+        noise=pltpu.VMEM((2, 32, STEPS), bf16),
+        clean=pltpu.VMEM((2, 32, STEPS), bf16),
+        input=pltpu.VMEM((32, 1024), bf16),
+        cot_in=pltpu.VMEM((STEPS, 2, 2048), bf16),
+        own_prefix=pltpu.VMEM((16, 512), bf16),
+        own_action=pltpu.VMEM((8, 512), bf16),
+        own_query=pltpu.VMEM((64, 256), bf16),
     )
     for part in range(3):
         scratch[f"weight_{part}"] = pltpu.VMEM((2, 4, 4, 4, 16, 256), bf16)
@@ -711,7 +746,7 @@
             jax.ShapeDtypeStruct((16, 512), f32),
             jax.ShapeDtypeStruct((8, 512), f32),
         ),
-        in_specs=[smem] * 3 + [pl.BlockSpec(memory_space=pl.ANY)] + [vmem] * 9,
+        in_specs=[hbm] * 11 + [vmem] * 2,
         out_specs=(vmem,) * 4,
         scratch_shapes=[scratch],
         compiler_params=pltpu.CompilerParams(
@@ -722,8 +757,15 @@
         ),
         name="step",
     )(
-        cameras, text_length, flow_time, hidden, noise, clean, sine, cosine, input_weight, cot,
-        own_prefix, own_action, own_query,
+        *[
+            pltpu.with_memory_space_constraint(operand, pltpu.HBM)
+            for operand in (
+                cameras, text_length, flow_time, hidden, noise, clean, input_weight, cot,
+                own_prefix, own_action, own_query,
+            )
+        ],
+        sine,
+        cosine,
     )
 
 
@@ -756,13 +798,13 @@
         prefix_hidden,
         action_noise.transpose(0, 2, 1),
         clean_actions.transpose(0, 2, 1),
-        sine,
-        cosine,
         input_weight,
         cotangent.transpose(1, 0, 2),
         prefix_kv_weight,
         action_kv_weight,
         query_weight,
+        sine,
+        cosine,
     )
 
 

time: 97.3 us -> 86.8 us (0.89)
  local copies, waits for them, and re-layouts: 10.4 us -> 3.02 us
  Pallas kernels: 84.9 us -> 82.2 us
    unnamed x23 -> x3, local copies, waits for them, and re-layouts: 9.25 us -> 1.85 us
    pallas_call x1, Pallas kernels: 84.9 us -> 82.2 us  [step(): pl.pallas_call(step_kernel, out_shape=(jax.ShapeDtypeStruct((2, STEPS, 20...]
where the time goes in v4:
time: 86.8 us; the launch traced here: 86.6 us
  Pallas kernels  82.2 us (95%)
  local copies, waits for them, and re-layouts  3.02 us (3%)
    pallas_call x1, Pallas kernels, step(): pl.pallas_call(step_kernel, out_shape=(jax.ShapeDtypeStruct((2, STEPS, 20...  82.2 us
    unnamed x3, local copies, waits for them, and re-layouts  1.85 us

profile of v4, /device:TPU:0, one launch (start us, length us, event | category | flops | bytes accessed | tf_op | source)
XLA Modules:
  0.0 86.6 jit_solution(16241502683137198559)
XLA Ops:
  0.6 0.8 multiply_cosine_fusion
  1.4 82.2 %step.1 = (bf16[2,50,2048]{2,1,0:T(8,128)(2,1)S(1)}, f32[64,256]{1,0:T(8,128)S(1)}, f32[16,512]{1,0:T(8,128)S(1)}, f32[8,512]{1,0:T(8,128)S(1)}) custom-call(s32[2]{0:T(128)} %cameras_hbm.1, s32[2]{0:T(128)} %text_hbm.1, f32[2]{0:T(128)} %flow_hbm.1, bf16[2,816,2048]{2,1,0:T(8,128)(2,1)} %hidden_hbm.1, bf16[2,32,50]{2,1,0:T(8,128)(2,1)} %bitcast.4, ...), custom_call_target="tpu_custom_call" | custom-call | flops 10000000000 | bytes 9000000 | tf_op jit(solution)/shard_map/step/pallas_call | solution.py:741
  83.6 1.2 %copy.15 = bf16[2,50,2048]{2,0,1:T(2,128)(2,1)} copy(bf16[2,50,2048]{2,1,0:T(8,128)(2,1)S(1)} %get-tuple-element.4) | data formatting | bytes 819200 | tf_op jit(solution)/shard_map/step/pallas_call | solution.py:741
  84.8 0.6 copy.19
  85.4 0.6 copy.20
  86.0 0.6 copy.21
  (1 shorter events, 0.0 us)

commit v5 on v4

--- a/solution.py
+++ b/solution.py
@@ -533,16 +533,37 @@
         kv[start : start + PAD_STEPS, 0:256] = keys[rows]
         kv[start : start + PAD_STEPS, 256:512] = values[rows]
 
+    low_ref, ds_ref, gkv = v["low"], v["ds"], v["gkv"]
+
+    def sixteenth(rows):
+        return (rows.astype(f32) * 0.0625).astype(bf16)
+
+    def turn_pairs(rows, turned):
+        first = lax.broadcasted_iota(jnp.int32, (256, 128), 1) < 64
+        across = lanes_dot(eye[...], rows)
+        for h in range(8):
+            pair = across[:, (h // 2) * 128 : (h // 2 + 1) * 128]
+            keep = first if h % 2 == 0 else jnp.logical_not(first)
+            turned[h] = jnp.where(keep, pair, 0.0).astype(bf16)
+
+    for s in range(2):
+        cot = v["cot"][:, s * PAD_STEPS : (s + 1) * PAD_STEPS, :].reshape(512, 256)
+        turn_pairs(cot, v["cot_t"].at[s])
+    fetches["cameras"].wait()
+    fetches["text"].wait()
     for offset in range(1, 8):
         member = place.group_member(offset, -1)
         links.arrived(v["query"].at[member], (place.dp, member), exchange + offset)
 
-    fetches["cameras"].wait()
-    fetches["text"].wait()
-    low_ref, ds_ref, gkv = v["low"], v["ds"], v["gkv"]
-
-    def sixteenth(rows):
-        return (rows.astype(f32) * 0.0625).astype(bf16)
+    returns = links.slots(16)
+
+    def return_op(s, offset):
+        member = place.group_member(offset)
+        mine = pl.ds(pl.multiple_of(s * PAD_STEPS, PAD_STEPS), PAD_STEPS)
+        return links.op(
+            v["gq"].at[member, mine], v["group_gq"].at[seq, mine], (place.dp, member),
+            returns + s * 8 + offset,
+        )
 
     def sample(s, carry):
         length = v["cameras"][s] * IMG + v["text"][s]
@@ -562,22 +583,17 @@
         inner = jnp.sum(probs * dprob, axis=-1, keepdims=True)
         ds_ref[...] = (probs * (dprob - inner)).astype(bf16)
         v["gq"][:, mine, :] = dot(ds_ref[...], kv[tokens, 0:256]).astype(bf16).reshape(8, 64, 256)
+        for offset in range(1, 8):
+            return_op(s, offset).start()
         attended = dot(low_ref[...], kv[tokens, 256:512]).astype(bf16)
         for h in range(8):
             attended_ref[s, :, h * 256 : (h + 1) * 256] = attended[h * 64 : h * 64 + STEPS]
-
-        first = lax.broadcasted_iota(jnp.int32, (256, 128), 1) < 64
-        for rows, turned in ((query, v["query_t"]), (cot, v["cot_t"])):
-            across = lanes_dot(eye[...], rows)
-            for h in range(8):
-                pair = across[:, (h // 2) * 128 : (h // 2 + 1) * 128]
-                keep = first if h % 2 == 0 else jnp.logical_not(first)
-                turned[h] = jnp.where(keep, pair, 0.0).astype(bf16)
+        turn_pairs(query, v["query_t"])
 
         def tile(begin, width):
             at = pl.ds(begin, width)
             to = pl.ds(pl.multiple_of(start + begin, 128), width)
-            for left, right, top in ((v["query_t"], ds_ref, 0), (v["cot_t"], low_ref, 256)):
+            for left, right, top in ((v["query_t"], ds_ref, 0), (v["cot_t"].at[s], low_ref, 256)):
                 total = jnp.zeros((256, width), f32)
                 for h in range(8):
                     term = dot(left[h], right[(h // 2) * 128 : (h // 2 + 1) * 128, at])
@@ -594,11 +610,6 @@
 
     lax.fori_loop(0, 2, sample, 0)
 
-    for offset in range(1, 8):
-        member = place.group_member(offset)
-        links.go(
-            v["gq"].at[member], v["group_gq"].at[seq], (place.dp, member), exchange + 8 + offset
-        )
     v["group_gq"][seq] = v["gq"][seq]
 
     for s in range(2):
@@ -628,11 +639,14 @@
         pair_op(k).start()
         return carry
 
-    lax.fori_loop(0, 8, grad_prefix, 0, unroll=2)
     def grad_query():
         for offset in range(1, 8):
             member = place.group_member(offset, -1)
-            links.arrived(v["group_gq"].at[member], (place.dp, member), exchange + 8 + offset)
+            for s in range(2):
+                mine = slice(s * PAD_STEPS, (s + 1) * PAD_STEPS)
+                links.arrived(
+                    v["group_gq"].at[member, mine], (place.dp, member), returns + s * 8 + offset
+                )
         rows = v["group_gq"][...].reshape(1024, 256)
         for a in range(4):
             value = dot(act_t[a * 256 : (a + 1) * 256, :], rows)
@@ -653,7 +667,13 @@
             pair_op(k).wait_recv()
         yield
 
-    works = [reduce_query(links, place, grad_query, v, out_query_ref), paired()]
+    query_work = reduce_query(links, place, grad_query, v, out_query_ref)
+    lax.fori_loop(0, 4, grad_prefix, 0, unroll=2)
+    next(query_work)
+    lax.fori_loop(4, 6, grad_prefix, 0)
+    next(query_work)
+    lax.fori_loop(6, 8, grad_prefix, 0)
+    works = [query_work, paired()]
     works += [reduce_part(links, place, grad, pair, v, part, finish(part)) for part in range(3)]
     early = list(links.sent)
     links.sent.clear()
@@ -668,6 +688,9 @@
     run_together(works, [drain(early[i::4]) for i in range(4)])
     for op in links.sent:
         op.wait_send()
+    for offset in range(1, 8):
+        for s in range(2):
+            return_op(s, offset).wait_send()
     for k in range(8):
         pair_op(k).wait_send()
 
@@ -702,7 +725,7 @@
         low=pltpu.VMEM((512, KEYS), bf16),
         ds=pltpu.VMEM((512, KEYS), bf16),
         query_t=pltpu.VMEM((8, 256, 128), bf16),
-        cot_t=pltpu.VMEM((8, 256, 128), bf16),
+        cot_t=pltpu.VMEM((2, 8, 256, 128), bf16),
         gkv=pltpu.VMEM((512, 2 * KEYS), bf16),
         grad=pltpu.VMEM((4, 2, 2, 2, 4, ROWS, 256), f32),
         pair=pltpu.VMEM((4, 4, 4, ROWS, 256), f32),

time: 86.8 us -> 89.1 us (1.026)
  Pallas kernels: 82.2 us -> 84.5 us
    pallas_call x1, Pallas kernels: 82.2 us -> 84.5 us  [step(): pl.pallas_call(step_kernel, out_shape=(jax.ShapeDtypeStruct((2, STEPS, 20...]
where the time goes in v5:
time: 89.1 us; the launch traced here: 89 us
  Pallas kernels  84.5 us (95%)
  local copies, waits for them, and re-layouts  3.02 us (3%)
    pallas_call x1, Pallas kernels, step(): pl.pallas_call(step_kernel, out_shape=(jax.ShapeDtypeStruct((2, STEPS, 20...  84.5 us
    unnamed x3, local copies, waits for them, and re-layouts  1.85 us

profile of v5, /device:TPU:0, one launch (start us, length us, event | category | flops | bytes accessed | tf_op | source)
XLA Modules:
  0.0 89.0 jit_solution(11506038987425812834)
XLA Ops:
  0.6 0.8 multiply_cosine_fusion
  1.4 84.5 %step.1 = (bf16[2,50,2048]{2,1,0:T(8,128)(2,1)S(1)}, f32[64,256]{1,0:T(8,128)S(1)}, f32[16,512]{1,0:T(8,128)S(1)}, f32[8,512]{1,0:T(8,128)S(1)}) custom-call(s32[2]{0:T(128)} %cameras_hbm.1, s32[2]{0:T(128)} %text_hbm.1, f32[2]{0:T(128)} %flow_hbm.1, bf16[2,816,2048]{2,1,0:T(8,128)(2,1)} %hidden_hbm.1, bf16[2,32,50]{2,1,0:T(8,128)(2,1)} %bitcast.4, ...), custom_call_target="tpu_custom_call" | custom-call | flops 10000000000 | bytes 9000000 | tf_op jit(solution)/shard_map/step/pallas_call | solution.py:764
  86.0 1.2 %copy.15 = bf16[2,50,2048]{2,0,1:T(2,128)(2,1)} copy(bf16[2,50,2048]{2,1,0:T(8,128)(2,1)S(1)} %get-tuple-element.4) | data formatting | bytes 819200 | tf_op jit(solution)/shard_map/step/pallas_call | solution.py:764
  87.2 0.6 copy.19
  87.8 0.6 copy.20
  88.4 0.6 copy.21
  (1 shorter events, 0.0 us)

commit v6 on v5

--- a/solution.py
+++ b/solution.py
@@ -344,8 +344,8 @@
         load.start()
         loads.append(load)
 
-    query_weight = v["query_weight"]
-    for name in ("flow", "noise", "clean", "own_prefix", "own_action", "own_query"):
+    query_weight, eye = v["query_weight"], v["eye"]
+    for name in ("own_prefix", "own_action", "own_query"):
         fetches[name].wait()
     own_prefix = v["own_prefix"]
     own_action = v["own_action"][...].astype(f32)
@@ -355,32 +355,32 @@
         at = place.at
         v[f"weight_{part}"][core, at[third], at[second], at[first]] = own_parts[part]
     query_weight[y, z_hi, core] = v["own_query"][...]
-    own_noisy = v["own_noisy"]
-    noisy = []
-    for s in range(2):
-        t = v["flow"][s]
-        noisy.append(t * v["noise"][s].astype(f32) + (1.0 - t) * v["clean"][s].astype(f32))
-    blank = jnp.zeros((32, PAD_STEPS - STEPS), f32)
-    own_noisy[...] = jnp.concatenate([noisy[0], blank, noisy[1], blank], axis=1).astype(bf16)
-    v["noisy"][seq] = own_noisy[...]
-    own_time = v["own_time"]
-    own_time[:, 0:512] = sin_ref[...]
-    own_time[:, 512:1024] = cos_ref[...]
-    v["time"][seq] = own_time[...]
     place.meet()
-
-    eye = v["eye"]
-    row = lax.broadcasted_iota(jnp.int32, (256, 256), 0)
-    col = lax.broadcasted_iota(jnp.int32, (256, 256), 1)
-    eye[...] = jnp.where(row == col, 1.0, 0.0).astype(bf16)
 
     packet = links.slots(16)
     def send_packets():
+        for name in ("flow", "noise", "clean"):
+            fetches[name].wait()
+        own_noisy = v["own_noisy"]
+        noisy = []
+        for s in range(2):
+            t = v["flow"][s]
+            noisy.append(t * v["noise"][s].astype(f32) + (1.0 - t) * v["clean"][s].astype(f32))
+        blank = jnp.zeros((32, PAD_STEPS - STEPS), f32)
+        own_noisy[...] = jnp.concatenate([noisy[0], blank, noisy[1], blank], axis=1).astype(bf16)
+        v["noisy"][seq] = own_noisy[...]
+        own_time = v["own_time"]
+        own_time[:, 0:512] = sin_ref[...]
+        own_time[:, 512:1024] = cos_ref[...]
+        v["time"][seq] = own_time[...]
         for offset in range(1, 8):
             to = (place.dp, place.group_member(offset))
             links.go(own_noisy, v["noisy"].at[seq], to, packet + offset)
             links.go(own_time, v["time"].at[seq], to, packet + 8 + offset)
         fetches["input"].wait()
+        row = lax.broadcasted_iota(jnp.int32, (256, 256), 0)
+        col = lax.broadcasted_iota(jnp.int32, (256, 256), 1)
+        eye[...] = jnp.where(row == col, 1.0, 0.0).astype(bf16)
 
     act, act_t = v["act"], v["act_t"]
 
@@ -474,12 +474,14 @@
             rows = slice(half * 512, (half + 1) * 512)
             value = dot(act[rows, :], wide).astype(bf16)
             v["query_out"][half * 4 : half * 4 + 4] = value.reshape(4, 128, 256)
-        for offset in range(1, 8):
-            member = place.group_member(offset)
-            links.go(
-                v["query_out"].at[member], v["query"].at[seq], (place.dp, member),
-                exchange + offset,
-            )
+        for s in range(2):
+            mine = slice(s * PAD_STEPS, (s + 1) * PAD_STEPS)
+            for offset in (2, 6, 1, 3, 5, 7, 4):
+                member = place.group_member(offset)
+                links.go(
+                    v["query_out"].at[member, mine], v["query"].at[seq, mine],
+                    (place.dp, member), exchange + s * 8 + offset,
+                )
         v["query"][seq] = v["query_out"][seq]
 
     works = [gather_query(links, place, query_weight, send_queries)]
@@ -551,10 +553,6 @@
         turn_pairs(cot, v["cot_t"].at[s])
     fetches["cameras"].wait()
     fetches["text"].wait()
-    for offset in range(1, 8):
-        member = place.group_member(offset, -1)
-        links.arrived(v["query"].at[member], (place.dp, member), exchange + offset)
-
     returns = links.slots(16)
 
     def return_op(s, offset):
@@ -573,6 +571,11 @@
         column = lax.broadcasted_iota(jnp.int32, (1, KEYS), 1)
         valid = (column < length) | ((column >= PREFIX) & (column < PREFIX + STEPS))
         bias = jnp.where(valid, 0.0, -1e30)
+        for offset in range(1, 8):
+            member = place.group_member(offset, -1)
+            links.arrived(
+                v["query"].at[member, mine], (place.dp, member), exchange + s * 8 + offset
+            )
         query = v["query"][:, mine, :].reshape(512, 256)
         cot = v["cot"][:, mine, :].reshape(512, 256)
         logits = lanes_dot(sixteenth(query), kv[tokens, 0:256]) + bias
@@ -667,12 +670,8 @@
             pair_op(k).wait_recv()
         yield
 
+    lax.fori_loop(0, 8, grad_prefix, 0, unroll=2)
     query_work = reduce_query(links, place, grad_query, v, out_query_ref)
-    lax.fori_loop(0, 4, grad_prefix, 0, unroll=2)
-    next(query_work)
-    lax.fori_loop(4, 6, grad_prefix, 0)
-    next(query_work)
-    lax.fori_loop(6, 8, grad_prefix, 0)
     works = [query_work, paired()]
     works += [reduce_part(links, place, grad, pair, v, part, finish(part)) for part in range(3)]
     early = list(links.sent)

time: 89.1 us -> 88.3 us (level)
  no operation moved by 1% of the time
where the time goes in v6:
time: 88.3 us; the launch traced here: 88.2 us
  Pallas kernels  83.7 us (95%)
  local copies, waits for them, and re-layouts  3.02 us (3%)
    pallas_call x1, Pallas kernels, step(): pl.pallas_call(step_kernel, out_shape=(jax.ShapeDtypeStruct((2, STEPS, 20...  83.7 us
    unnamed x3, local copies, waits for them, and re-layouts  1.85 us

profile of v6, /device:TPU:0, one launch (start us, length us, event | category | flops | bytes accessed | tf_op | source)
XLA Modules:
  0.0 88.2 jit_solution(18219793902422102548)
XLA Ops:
  0.6 0.8 multiply_cosine_fusion
  1.4 83.7 %step.1 = (bf16[2,50,2048]{2,1,0:T(8,128)(2,1)S(1)}, f32[64,256]{1,0:T(8,128)S(1)}, f32[16,512]{1,0:T(8,128)S(1)}, f32[8,512]{1,0:T(8,128)S(1)}) custom-call(s32[2]{0:T(128)} %cameras_hbm.1, s32[2]{0:T(128)} %text_hbm.1, f32[2]{0:T(128)} %flow_hbm.1, bf16[2,816,2048]{2,1,0:T(8,128)(2,1)} %hidden_hbm.1, bf16[2,32,50]{2,1,0:T(8,128)(2,1)} %bitcast.4, ...), custom_call_target="tpu_custom_call" | custom-call | flops 10000000000 | bytes 9000000 | tf_op jit(solution)/shard_map/step/pallas_call | solution.py:763
  85.2 1.2 %copy.15 = bf16[2,50,2048]{2,0,1:T(2,128)(2,1)} copy(bf16[2,50,2048]{2,1,0:T(8,128)(2,1)S(1)} %get-tuple-element.4) | data formatting | bytes 819200 | tf_op jit(solution)/shard_map/step/pallas_call | solution.py:763
  86.3 0.6 copy.19
  87.0 0.6 copy.20
  87.6 0.6 copy.21
  (1 shorter events, 0.0 us)

commit v7 on v6

--- a/solution.py
+++ b/solution.py
@@ -10,7 +10,7 @@
 IMG = 256
 EPS = 1e-06
 MESH = pl.DeviceIdType.MESH
-VMEM_LIMIT = 50 * 1024 * 1024
+VMEM_LIMIT = 52 * 1024 * 1024
 PREFIX, STEPS, PAD_STEPS, KEYS = 816, 50, 64, 896
 
 ROWS = 48
@@ -104,7 +104,7 @@
 
 def direct(links, place, axis, view, slot):
     own = place.at[axis]
-    for by in (1, 3, 2):
+    for by in (2, 1, 3):
         to = place.device(**{axis: place.shifted(axis, by)})
         links.go(view(own), view(own), to, slot + by - 1)
     yield
@@ -115,19 +115,23 @@
 def ring(links, place, axis, view, slot, landed):
     own, right, left, across = (place.shifted(axis, by) for by in (0, 1, 3, 2))
     to_right, to_left = (place.device(**{axis: at}) for at in (right, left))
-    links.go(view(own), view(own), to_right, slot)
-    links.go(view(own), view(own), to_left, slot + 1)
+    for half in (0, 1):
+        links.go(view(own, half), view(own, half), to_right, slot + half)
+        links.go(view(own, 1 - half), view(own, 1 - half), to_left, slot + 2 + half)
     landed(own)
     yield
-    links.arrived(view(left), to_right, slot)
-    links.go(view(left, 0), view(left, 0), to_right, slot + 2)
-    links.arrived(view(right), to_left, slot + 1)
-    links.go(view(right, 1), view(right, 1), to_left, slot + 3)
+    links.arrived(view(left, 0), to_right, slot)
+    links.go(view(left, 0), view(left, 0), to_right, slot + 4)
+    links.arrived(view(right, 1), to_left, slot + 2)
+    links.go(view(right, 1), view(right, 1), to_left, slot + 5)
+    yield
+    links.arrived(view(left, 1), to_right, slot + 1)
     landed(left)
+    links.arrived(view(right, 0), to_left, slot + 3)
     landed(right)
     yield
-    links.arrived(view(across, 0), to_right, slot + 2)
-    links.arrived(view(across, 1), to_left, slot + 3)
+    links.arrived(view(across, 0), to_right, slot + 4)
+    links.arrived(view(across, 1), to_left, slot + 5)
     landed(across)
 
 
@@ -151,7 +155,7 @@
 def gather_part(links, place, ref, order):
     core = place.core
     first, second, third = order
-    slot = links.slots(10)
+    slot = links.slots(12)
     at = place.at
     yield from direct(
         links, place, first, lambda block: ref.at[core, at[third], at[second], block], slot
@@ -169,7 +173,7 @@
 
 def gather_query(links, place, query_ref, then):
     core, y, z_hi = place.core, place.at["y"], place.z_hi
-    slot = links.slots(5)
+    slot = links.slots(7)
     links.go(query_ref.at[y, z_hi, core], query_ref.at[y, z_hi, core], place.z_far, slot)
     yield
     links.arrived(query_ref.at[y, 1 - z_hi, core], place.z_far, slot)
@@ -474,14 +478,12 @@
             rows = slice(half * 512, (half + 1) * 512)
             value = dot(act[rows, :], wide).astype(bf16)
             v["query_out"][half * 4 : half * 4 + 4] = value.reshape(4, 128, 256)
-        for s in range(2):
-            mine = slice(s * PAD_STEPS, (s + 1) * PAD_STEPS)
-            for offset in (2, 6, 1, 3, 5, 7, 4):
-                member = place.group_member(offset)
-                links.go(
-                    v["query_out"].at[member, mine], v["query"].at[seq, mine],
-                    (place.dp, member), exchange + s * 8 + offset,
-                )
+        for offset in (2, 6, 1, 3, 5, 7, 4):
+            member = place.group_member(offset)
+            links.go(
+                v["query_out"].at[member], v["query"].at[seq], (place.dp, member),
+                exchange + offset,
+            )
         v["query"][seq] = v["query_out"][seq]
 
     works = [gather_query(links, place, query_weight, send_queries)]
@@ -553,15 +555,9 @@
         turn_pairs(cot, v["cot_t"].at[s])
     fetches["cameras"].wait()
     fetches["text"].wait()
-    returns = links.slots(16)
-
-    def return_op(s, offset):
-        member = place.group_member(offset)
-        mine = pl.ds(pl.multiple_of(s * PAD_STEPS, PAD_STEPS), PAD_STEPS)
-        return links.op(
-            v["gq"].at[member, mine], v["group_gq"].at[seq, mine], (place.dp, member),
-            returns + s * 8 + offset,
-        )
+    for offset in range(1, 8):
+        member = place.group_member(offset, -1)
+        links.arrived(v["query"].at[member], (place.dp, member), exchange + offset)
 
     def sample(s, carry):
         length = v["cameras"][s] * IMG + v["text"][s]
@@ -571,11 +567,6 @@
         column = lax.broadcasted_iota(jnp.int32, (1, KEYS), 1)
         valid = (column < length) | ((column >= PREFIX) & (column < PREFIX + STEPS))
         bias = jnp.where(valid, 0.0, -1e30)
-        for offset in range(1, 8):
-            member = place.group_member(offset, -1)
-            links.arrived(
-                v["query"].at[member, mine], (place.dp, member), exchange + s * 8 + offset
-            )
         query = v["query"][:, mine, :].reshape(512, 256)
         cot = v["cot"][:, mine, :].reshape(512, 256)
         logits = lanes_dot(sixteenth(query), kv[tokens, 0:256]) + bias
@@ -586,8 +577,6 @@
         inner = jnp.sum(probs * dprob, axis=-1, keepdims=True)
         ds_ref[...] = (probs * (dprob - inner)).astype(bf16)
         v["gq"][:, mine, :] = dot(ds_ref[...], kv[tokens, 0:256]).astype(bf16).reshape(8, 64, 256)
-        for offset in range(1, 8):
-            return_op(s, offset).start()
         attended = dot(low_ref[...], kv[tokens, 256:512]).astype(bf16)
         for h in range(8):
             attended_ref[s, :, h * 256 : (h + 1) * 256] = attended[h * 64 : h * 64 + STEPS]
@@ -613,6 +602,11 @@
 
     lax.fori_loop(0, 2, sample, 0)
 
+    for offset in (2, 6, 1, 3, 5, 7, 4):
+        member = place.group_member(offset)
+        links.go(
+            v["gq"].at[member], v["group_gq"].at[seq], (place.dp, member), exchange + 8 + offset
+        )
     v["group_gq"][seq] = v["gq"][seq]
 
     for s in range(2):
@@ -627,10 +621,14 @@
             grad.at[a, b, 1 - core], pair.at[a, pl.ds(b * 2, 2)], place.sibling, pairing + k
         )
 
-    def grad_prefix(k, carry):
+    def multiply(k):
         at = pl.ds(pl.multiple_of(k * 256, 256), 256)
-        a, b = k // 2, lax.rem(k, 2)
-        value = dot(gkv[...], norm[:, at])
+        v["product"][lax.rem(k, 2)] = dot(gkv[...], norm[:, at])
+
+    def deliver(k):
+        at = pl.ds(pl.multiple_of(k * 256, 256), 256)
+        a, b = lax.div(k, 2), lax.rem(k, 2)
+        value = v["product"][b]
         high = value.astype(bf16)
         low = (value - high.astype(f32)).astype(bf16)
         value = lanes_dot(eye[...], high) + lanes_dot(eye[...], low)
@@ -640,16 +638,20 @@
         action += dot(v["right_t"][at, :], ds_ref[0:128, 256:512])
         grad[a, b, :, :, :, 32:48, :] = action.reshape(2, 2, 4, 16, 256)
         pair_op(k).start()
+
+    def grad_prefix(k, carry):
+        deliver(k - 1)
+        multiply(k)
         return carry
+
+    multiply(0)
+    lax.fori_loop(1, 8, grad_prefix, 0)
+    deliver(7)
 
     def grad_query():
         for offset in range(1, 8):
             member = place.group_member(offset, -1)
-            for s in range(2):
-                mine = slice(s * PAD_STEPS, (s + 1) * PAD_STEPS)
-                links.arrived(
-                    v["group_gq"].at[member, mine], (place.dp, member), returns + s * 8 + offset
-                )
+            links.arrived(v["group_gq"].at[member], (place.dp, member), exchange + 8 + offset)
         rows = v["group_gq"][...].reshape(1024, 256)
         for a in range(4):
             value = dot(act_t[a * 256 : (a + 1) * 256, :], rows)
@@ -670,7 +672,6 @@
             pair_op(k).wait_recv()
         yield
 
-    lax.fori_loop(0, 8, grad_prefix, 0, unroll=2)
     query_work = reduce_query(links, place, grad_query, v, out_query_ref)
     works = [query_work, paired()]
     works += [reduce_part(links, place, grad, pair, v, part, finish(part)) for part in range(3)]
@@ -687,9 +688,6 @@
     run_together(works, [drain(early[i::4]) for i in range(4)])
     for op in links.sent:
         op.wait_send()
-    for offset in range(1, 8):
-        for s in range(2):
-            return_op(s, offset).wait_send()
     for k in range(8):
         pair_op(k).wait_send()
 
@@ -728,6 +726,7 @@
         gkv=pltpu.VMEM((512, 2 * KEYS), bf16),
         grad=pltpu.VMEM((4, 2, 2, 2, 4, ROWS, 256), f32),
         pair=pltpu.VMEM((4, 4, 4, ROWS, 256), f32),
+        product=pltpu.VMEM((2, 512, 256), f32),
         grad_query=pltpu.VMEM((4, 2, 2, 64, 256), f32),
         query_pair=pltpu.VMEM((4, 2, 64, 256), f32),
         query_wire=pltpu.VMEM((4, 2, 64, 256), bf16),

time: 88.3 us -> 80.5 us (0.912)
  Pallas kernels: 83.7 us -> 75.9 us
    pallas_call x1, Pallas kernels: 83.7 us -> 75.9 us  [step(): pl.pallas_call(step_kernel, out_shape=(jax.ShapeDtypeStruct((2, STEPS, 20...]
where the time goes in v7:
time: 80.5 us; the launch traced here: 80.4 us
  Pallas kernels  75.9 us (94%)
  local copies, waits for them, and re-layouts  3.02 us (4%)
  other arithmetic  0.82 us (1%)
    pallas_call x1, Pallas kernels, step(): pl.pallas_call(step_kernel, out_shape=(jax.ShapeDtypeStruct((2, STEPS, 20...  75.9 us
    unnamed x3, local copies, waits for them, and re-layouts  1.85 us

profile of v7, /device:TPU:0, one launch (start us, length us, event | category | flops | bytes accessed | tf_op | source)
XLA Modules:
  0.0 80.4 jit_solution(1272190212582151188)
XLA Ops:
  0.6 0.8 multiply_cosine_fusion
  1.4 75.9 %step.1 = (bf16[2,50,2048]{2,1,0:T(8,128)(2,1)S(1)}, f32[64,256]{1,0:T(8,128)S(1)}, f32[16,512]{1,0:T(8,128)S(1)}, f32[8,512]{1,0:T(8,128)S(1)}) custom-call(s32[2]{0:T(128)} %cameras_hbm.1, s32[2]{0:T(128)} %text_hbm.1, f32[2]{0:T(128)} %flow_hbm.1, bf16[2,816,2048]{2,1,0:T(8,128)(2,1)} %hidden_hbm.1, bf16[2,32,50]{2,1,0:T(8,128)(2,1)} %bitcast.4, ...), custom_call_target="tpu_custom_call" | custom-call | flops 10000000000 | bytes 9000000 | tf_op jit(solution)/shard_map/step/pallas_call | solution.py:762
  77.3 1.2 %copy.15 = bf16[2,50,2048]{2,0,1:T(2,128)(2,1)} copy(bf16[2,50,2048]{2,1,0:T(8,128)(2,1)S(1)} %get-tuple-element.4) | data formatting | bytes 819200 | tf_op jit(solution)/shard_map/step/pallas_call | solution.py:762
  78.5 0.6 copy.19
  79.1 0.6 copy.20
  79.8 0.6 copy.21
  (1 shorter events, 0.0 us)

commit v8 on v7

--- a/solution.py
+++ b/solution.py
@@ -214,9 +214,10 @@
     links.arrived(fulls(1, 1), to_left, slot + 5)
 
 
-def reduce_direct(links, place, axis, block_of, landing, slot):
+def reduce_direct(links, place, axis, block_of, landing, slot, ready=lambda block: None):
     for by in (2, 1, 3):
         block = place.shifted(axis, by)
+        ready(block)
         links.go(
             block_of(block), landing.at[by - 1], place.device(**{axis: block}), slot + by - 1
         )
@@ -250,19 +251,25 @@
         links, place, first, pack, lambda block, side: wire.at[block, HALVES[side]], half,
         lambda way, side: full.at[way, HALVES[side]], slot,
     )
-    total, wire2, full2 = (v[f"{name}2_{part}"] for name in ("sum", "wire", "full"))
-    for i in range(4):
+    wire2, full2 = v[f"wire2_{part}"], v[f"full2_{part}"]
+
+    def summed(i, j):
+        value = mine(place.at[first], i, j)
+        return value + full[0, i, j].astype(f32) + full[1, i, j].astype(f32)
+
+    def ready(block):
         for j in range(4):
-            value = mine(place.at[first], i, j)
-            value = value + full[0, i, j].astype(f32) + full[1, i, j].astype(f32)
-            total[i, j] = value
-            wire2[i, j] = value.astype(bf16)
-    yield from reduce_direct(links, place, second, lambda block: wire2.at[block], full2, slot + 6)
+            wire2[block, j] = summed(block, j).astype(bf16)
+
+    yield from reduce_direct(
+        links, place, second, lambda block: wire2.at[block], full2, slot + 6, ready
+    )
     total3, full3 = v[f"sum3_{part}"], v[f"full3_{part}"]
-    value = total[place.at[second]]
-    for k in range(3):
-        value = value + full2[k].astype(f32)
-    total3[...] = value
+    for j in range(4):
+        value = summed(place.at[second], j)
+        for k in range(3):
+            value = value + full2[k, j].astype(f32)
+        total3[j] = value
     yield from reduce_direct(links, place, third, lambda block: total3.at[block], full3, slot + 9)
     finish(total3[place.at[third]] + full3[0] + full3[1] + full3[2])
 
@@ -522,7 +529,7 @@
         return keys + dot(v["left"][:, at], block), values + dot(v["right"][:, at], block)
 
     zero = jnp.zeros((2 * PAD_STEPS, 256), f32)
-    keys, values = lax.fori_loop(0, 8, unpack, (zero, zero))
+    keys, values = lax.fori_loop(0, 8, unpack, (zero, zero), unroll=4)
     keys, values = keys.astype(bf16), values.astype(bf16)
 
     def prefix(i, carry):
@@ -596,7 +603,7 @@
             tile(pl.multiple_of(t * 256, 256), 256)
             return carry
 
-        lax.fori_loop(0, 3, wide_tile, 0)
+        lax.fori_loop(0, 3, wide_tile, 0, unroll=3)
         tile(768, 128)
         return carry
 
@@ -754,7 +761,6 @@
         scratch[f"wire1_{part}"] = pltpu.VMEM((4, 4, 4, 16, 256), bf16)
         scratch[f"half1_{part}"] = pltpu.VMEM((2, 2, 4, 16, 256), bf16)
         scratch[f"full1_{part}"] = pltpu.VMEM((2, 4, 4, 16, 256), bf16)
-        scratch[f"sum2_{part}"] = pltpu.VMEM((4, 4, 16, 256), f32)
         scratch[f"wire2_{part}"] = pltpu.VMEM((4, 4, 16, 256), bf16)
         scratch[f"full2_{part}"] = pltpu.VMEM((3, 4, 16, 256), bf16)
         scratch[f"sum3_{part}"] = pltpu.VMEM((4, 16, 256), f32)

time: 80.5 us -> 78.5 us (0.975)
  Pallas kernels: 75.9 us -> 73.9 us
    pallas_call x1, Pallas kernels: 75.9 us -> 73.9 us  [step(): pl.pallas_call(step_kernel, out_shape=(jax.ShapeDtypeStruct((2, STEPS, 20...]
where the time goes in v8:
time: 78.5 us; the launch traced here: 78.4 us
  Pallas kernels  73.9 us (94%)
  local copies, waits for them, and re-layouts  3.02 us (4%)
  other arithmetic  0.82 us (1%)
    pallas_call x1, Pallas kernels, step(): pl.pallas_call(step_kernel, out_shape=(jax.ShapeDtypeStruct((2, STEPS, 20...  73.9 us
    unnamed x3, local copies, waits for them, and re-layouts  1.85 us

profile of v8, /device:TPU:0, one launch (start us, length us, event | category | flops | bytes accessed | tf_op | source)
XLA Modules:
  0.0 78.4 jit_solution(2447616059794233375)
XLA Ops:
  0.6 0.8 %multiply_cosine_fusion = (f32[2,512]{1,0:T(2,128)S(1)}, f32[2,512]{1,0:T(2,128)S(1)}) fusion(f32[512]{0:T(512)S(1)} %multiply_divide_fusion, f32[2]{0:T(128)} %flow_hbm.1), kind=kLoop, calls=%fused_computation | loop fusion | flops 1024 | bytes 10248 | tf_op jit(solution)/shard_map/cos | solution.py:804
  1.4 73.9 %step.1 = (bf16[2,50,2048]{2,1,0:T(8,128)(2,1)S(1)}, f32[64,256]{1,0:T(8,128)S(1)}, f32[16,512]{1,0:T(8,128)S(1)}, f32[8,512]{1,0:T(8,128)S(1)}) custom-call(s32[2]{0:T(128)} %cameras_hbm.1, s32[2]{0:T(128)} %text_hbm.1, f32[2]{0:T(128)} %flow_hbm.1, bf16[2,816,2048]{2,1,0:T(8,128)(2,1)} %hidden_hbm.1, bf16[2,32,50]{2,1,0:T(8,128)(2,1)} %bitcast.4, ...), custom_call_target="tpu_custom_call" | custom-call | flops 10000000000 | bytes 9000000 | tf_op jit(solution)/shard_map/step/pallas_call | solution.py:768
  75.4 1.2 %copy.15 = bf16[2,50,2048]{2,0,1:T(2,128)(2,1)} copy(bf16[2,50,2048]{2,1,0:T(8,128)(2,1)S(1)} %get-tuple-element.4) | data formatting | bytes 819200 | tf_op jit(solution)/shard_map/step/pallas_call | solution.py:768
  76.5 0.6 copy.19
  77.2 0.6 copy.20
  77.8 0.6 copy.21
  (1 shorter events, 0.0 us)

commit v9 on v8

--- a/solution.py
+++ b/solution.py
@@ -537,7 +537,7 @@
         kv[at, :] = dot(norm[at, :], wp[...]).astype(bf16)
         return carry
 
-    lax.fori_loop(0, 4, prefix, 0)
+    lax.fori_loop(0, 4, prefix, 0, unroll=2)
     for s in range(2):
         rows = slice(s * PAD_STEPS, (s + 1) * PAD_STEPS)
         start = s * KEYS + PREFIX
@@ -607,7 +607,7 @@
         tile(768, 128)
         return carry
 
-    lax.fori_loop(0, 2, sample, 0)
+    lax.fori_loop(0, 2, sample, 0, unroll=2)
 
     for offset in (2, 6, 1, 3, 5, 7, 4):
         member = place.group_member(offset)

time: 78.5 us -> 79.2 us (level)
  no operation moved by 1% of the time
where the time goes in v9:
time: 79.2 us; the launch traced here: 79.1 us
  Pallas kernels  74.6 us (94%)
  local copies, waits for them, and re-layouts  3.02 us (4%)
  other arithmetic  0.82 us (1%)
    pallas_call x1, Pallas kernels, step(): pl.pallas_call(step_kernel, out_shape=(jax.ShapeDtypeStruct((2, STEPS, 20...  74.6 us
    unnamed x3, local copies, waits for them, and re-layouts  1.85 us

profile of v9, /device:TPU:0, one launch (start us, length us, event | category | flops | bytes accessed | tf_op | source)
XLA Modules:
  0.0 79.1 jit_solution(7968163774322081457)
XLA Ops:
  0.6 0.8 %multiply_cosine_fusion = (f32[2,512]{1,0:T(2,128)S(1)}, f32[2,512]{1,0:T(2,128)S(1)}) fusion(f32[512]{0:T(512)S(1)} %multiply_divide_fusion, f32[2]{0:T(128)} %flow_hbm.1), kind=kLoop, calls=%fused_computation | loop fusion | flops 1024 | bytes 10248 | tf_op jit(solution)/shard_map/cos | solution.py:804
  1.4 74.6 %step.1 = (bf16[2,50,2048]{2,1,0:T(8,128)(2,1)S(1)}, f32[64,256]{1,0:T(8,128)S(1)}, f32[16,512]{1,0:T(8,128)S(1)}, f32[8,512]{1,0:T(8,128)S(1)}) custom-call(s32[2]{0:T(128)} %cameras_hbm.1, s32[2]{0:T(128)} %text_hbm.1, f32[2]{0:T(128)} %flow_hbm.1, bf16[2,816,2048]{2,1,0:T(8,128)(2,1)} %hidden_hbm.1, bf16[2,32,50]{2,1,0:T(8,128)(2,1)} %bitcast.4, ...), custom_call_target="tpu_custom_call" | custom-call | flops 10000000000 | bytes 9000000 | tf_op jit(solution)/shard_map/step/pallas_call | solution.py:768
  76.0 1.2 %copy.15 = bf16[2,50,2048]{2,0,1:T(2,128)(2,1)} copy(bf16[2,50,2048]{2,1,0:T(8,128)(2,1)S(1)} %get-tuple-element.4) | data formatting | bytes 819200 | tf_op jit(solution)/shard_map/step/pallas_call | solution.py:768
  77.2 0.6 copy.19
  77.8 0.6 copy.20
  78.4 0.6 copy.21
  (1 shorter events, 0.0 us)
